TPU v7x, 512 devices: a whole 4x8x8 slice. The times are simulated.
512 devices in a mesh: tm: 32 (over x_lo, y, core), height: 8 (over z), rep: 2 (over x_hi).
Axes of the slice: x: 4 (x_hi: 2, x_lo: 2; x = x_hi * 2 + x_lo), y: 8, z: 8, core: 2. Of those that a mesh axis runs over, the one named last changes fastest.
Arguments:
- queries: bfloat16 [384, 32, 8, 2048], P(('rep', 'tm'), 'height'), parts along dimension 0, may hold values from -6 to 6
- key_tokens: bfloat16 [384, 32, 8, 2048], P(('rep', 'tm'), 'height'), parts along dimension 0, may hold values from -6 to 6
- value_tokens: bfloat16 [384, 32, 8, 2048], P(('rep', 'tm'), 'height'), parts along dimension 0, may hold values from -6 to 6
- text_keys: bfloat16 [512, 2048], P(('rep', 'tm'), 'height'), parts along dimension 0, may hold values from -8 to 8
- text_values: bfloat16 [512, 2048], P(('rep', 'tm'), 'height'), parts along dimension 0, may hold values from -6 to 6
- text_length: int32 [2], P('rep'), parts along dimension 0, may hold values from 32 to 256
Outputs:
- attended: bfloat16 [384, 32, 8, 2048], P(('rep', 'tm'), 'height'), parts along dimension 0
There are 2 independent parts, one for each index of `rep`. A program takes and returns all parts, laid end to end along the dimension named above; each array names one. Nothing has to cross between parts.
All inputs are finite; a program needn't handle non-finite values.
Results may differ from a plain program's by a relative error of at most 0.005.
Values may be sent and summed in bfloat16 or wider, within the bound.
A program may use at most 64 MiB of HBM per device.

v0:
```python
import jax
import jax.numpy as jnp
from jax import lax
from jax.sharding import PartitionSpec as P

DH = 128
TH = 8


def from_behind(block, axis, distance):
    devices = range(lax.axis_size(axis))
    route = [(i - distance, i) for i in devices if i - distance in devices]
    return lax.ppermute(block, axis, route)


def text_step(carry, piece, query_split, text_length, score_scale):
    running_max, running_sum, running_acc = carry
    piece_keys, piece_values = piece
    count = piece_keys.shape[0]
    local_heads = query_split.shape[3]
    keys_split = piece_keys.reshape(count, local_heads, DH)
    values_float = piece_values.reshape(count, local_heads, DH).astype(jnp.float32)
    scores = (
        jnp.einsum("fhwgd,ngd->gfhwn", query_split, keys_split, preferred_element_type=jnp.float32)
        * score_scale
    )
    positions = jnp.arange(count, dtype=jnp.int32)
    scores = jnp.where(positions < text_length[0], scores, -jnp.inf)
    new_max = jnp.maximum(running_max, jnp.max(scores, -1))
    weights = jnp.exp(scores - new_max[..., None])
    running_sum = jnp.sum(weights, -1)
    running_acc = jnp.einsum("gfhwn,ngd->gfhwd", weights, values_float)
    return (new_max, running_sum, running_acc)


def per_device(queries, key_tokens, value_tokens, text_keys, text_values, text_length):
    frames, local_rows, columns, features = queries.shape
    groups = lax.axis_size("height")
    group_width = features // groups
    local_heads = group_width // DH
    score_scale = 1.0 / DH**0.5
    full_rows = groups * local_rows

    def to_heads(array):
        return array.reshape(frames, local_rows, columns, groups, group_width)

    def from_heads(array):
        return array.reshape(frames, full_rows, columns, group_width)

    moved = (
        lax.all_to_all(to_heads(queries), "height", split_axis=3, concat_axis=1, tiled=True),
        lax.all_to_all(to_heads(key_tokens), "height", split_axis=3, concat_axis=1, tiled=True),
        lax.all_to_all(to_heads(value_tokens), "height", split_axis=3, concat_axis=1, tiled=True),
    )
    query_heads = from_heads(moved[0])
    key_heads = from_heads(moved[1])
    value_heads = from_heads(moved[2])
    near_prev = from_behind((key_heads, value_heads), "tm", 1)
    near_next = from_behind((key_heads, value_heads), "tm", -1)
    padding = ((0, 0), (TH, TH), (0, 0), (0, 0))
    keys_window = jnp.pad(jnp.concatenate([near_prev[0], key_heads, near_next[0]], 0), padding)
    values_window = jnp.pad(jnp.concatenate([near_prev[1], value_heads, near_next[1]], 0), padding)
    query_split = query_heads.reshape(frames, full_rows, columns, local_heads, DH)
    stat_shape = (local_heads, frames, full_rows, columns)
    initial = (
        jnp.full(stat_shape, -1e30, jnp.float32),
        jnp.zeros(stat_shape, jnp.float32),
        jnp.zeros(stat_shape + (DH,), jnp.float32),
    )
    gathered = (
        lax.all_gather(text_keys, "tm", axis=0, tiled=True),
        lax.all_gather(text_values, "tm", axis=0, tiled=True),
    )
    text_max, text_sum, text_acc = text_step(
        initial, (gathered[0], gathered[1]), query_split, text_length, score_scale
    )
    time_tile = lax.axis_index("tm")
    time_tiles = lax.axis_size("tm")
    height_tiles = full_rows // TH
    window_tiles = jnp.arange(3, dtype=jnp.int32)
    time_index = time_tile - 1 + window_tiles
    time_ok = jnp.repeat((time_index >= 0) & (time_index < time_tiles), frames)

    def one_tile(height_tile):
        anchor = jnp.zeros((), jnp.int32)
        row_start = height_tile * TH
        query_block = lax.dynamic_slice(
            query_heads, (anchor, row_start, anchor, anchor), (frames, TH, columns, group_width)
        )
        starts = (anchor, height_tile * TH, anchor, anchor)
        key_block = lax.dynamic_slice(
            keys_window, starts, (3 * frames, 3 * TH, columns, group_width)
        )
        value_block = lax.dynamic_slice(
            values_window, starts, (3 * frames, 3 * TH, columns, group_width)
        )
        height_index = height_tile - 1 + window_tiles
        height_ok = jnp.repeat((height_index >= 0) & (height_index < height_tiles), TH)
        valid_keys = (
            time_ok[:, None, None] & height_ok[None, :, None] & jnp.ones((1, 1, columns), bool)
        ).reshape(-1)
        query_rows = query_block.reshape(-1, group_width)
        key_rows = key_block.reshape(-1, group_width)
        value_rows = value_block.reshape(-1, group_width)
        tile_max = lax.dynamic_slice_in_dim(text_max, row_start, TH, 2).reshape(local_heads, -1)
        tile_sum = lax.dynamic_slice_in_dim(text_sum, row_start, TH, 2).reshape(local_heads, -1)
        tile_acc = lax.dynamic_slice_in_dim(text_acc, row_start, TH, 2).reshape(local_heads, -1, DH)

        def one_head(inputs):
            head_number, head_max, head_sum, head_acc = inputs
            query_head = lax.dynamic_slice_in_dim(query_rows, head_number * DH, DH, 1)
            key_head = lax.dynamic_slice_in_dim(key_rows, head_number * DH, DH, 1)
            value_head = lax.dynamic_slice_in_dim(value_rows, head_number * DH, DH, 1)
            scores = (
                lax.dot_general(
                    query_head,
                    key_head,
                    (((1,), (1,)), ((), ())),
                    preferred_element_type=jnp.float32,
                )
                * score_scale
            )
            scores = jnp.where(valid_keys[None, :], scores, -jnp.inf)
            row_max = jnp.maximum(jnp.max(scores, -1), head_max)
            weights = jnp.exp(scores - row_max[:, None])
            factor = jnp.exp(head_max - row_max)
            denominator = head_sum * factor + jnp.sum(weights, -1)
            numerator = head_acc * factor[:, None] + jnp.dot(
                weights.astype(jnp.bfloat16), value_head, preferred_element_type=jnp.float32
            )
            return (numerator / denominator[:, None]).astype(jnp.bfloat16)

        per_head = lax.map(
            one_head, (jnp.arange(local_heads, dtype=jnp.int32), tile_max, tile_sum, tile_acc)
        )
        return jnp.transpose(per_head, (1, 0, 2)).reshape(frames, TH, columns, group_width)

    tile_results = lax.map(one_tile, jnp.arange(height_tiles, dtype=jnp.int32))
    attended_heads = jnp.transpose(tile_results, (1, 0, 2, 3, 4)).reshape(
        frames, full_rows, columns, 1, group_width
    )
    returned = lax.all_to_all(attended_heads, "height", split_axis=1, concat_axis=3, tiled=True)
    return returned.reshape(frames, local_rows, columns, features)


def solution(mesh):
    placed = (
        P(("rep", "tm"), "height", None, None),
        P(("rep", "tm"), "height", None, None),
        P(("rep", "tm"), "height", None, None),
        P(("rep", "tm"), "height"),
        P(("rep", "tm"), "height"),
        P("rep"),
    )
    return jax.shard_map(
        per_device,
        mesh=mesh,
        in_specs=placed,
        out_specs=P(("rep", "tm"), "height", None, None),
        check_vma=False,
    )
```

profile of v0, /device:TPU:1, one launch (start us, length us, event | category | flops | bytes accessed | tf_op | source)
XLA Modules:
  0.0 306.1 jit_solution(4985952840422515553)
XLA Ops:
  0.0 2.2 copy.91
  2.2 10.9 %all-to-all-start.2 = ((bf16[6,4,8,8,256]{4,2,1,0,3:T(8,128)(2,1)}), bf16[6,4,8,8,256]{4,2,1,0,3:T(8,128)(2,1)S(1)}, u32[]{:S(2)}, u32[]{:S(2)}) async-start(bf16[6,4,8,8,256]{4,2,1,0,3:T(8,128)(2,1)} %bitcast.71), calls=%async_computation.2 | async-start | bytes 1572864 | tf_op jit(solution)/shard_map/all_to_all | solution.py:53
  14.1 22.6 %all-to-all-done.2 = bf16[6,4,8,8,256]{4,2,1,0,3:T(8,128)(2,1)S(1)} async-done(((bf16[6,4,8,8,256]{4,2,1,0,3:T(8,128)(2,1)}), bf16[6,4,8,8,256]{4,2,1,0,3:T(8,128)(2,1)S(1)}, u32[]{:S(2)}, u32[]{:S(2)}) %all-to-all-start.2) | async-done | bytes 786464 | tf_op jit(solution)/shard_map/all_to_all | solution.py:53
  36.7 3.5 %all-to-all-start.1 = ((bf16[6,4,8,8,256]{4,2,1,0,3:T(8,128)(2,1)}), bf16[6,4,8,8,256]{4,2,1,0,3:T(8,128)(2,1)S(1)}, u32[]{:S(2)}, u32[]{:S(2)}) async-start(bf16[6,4,8,8,256]{4,2,1,0,3:T(8,128)(2,1)} %bitcast.72), calls=%async_computation.1 | async-start | bytes 1572864 | tf_op jit(solution)/shard_map/all_to_all | solution.py:52
  41.2 22.5 %all-to-all-done.1 = bf16[6,4,8,8,256]{4,2,1,0,3:T(8,128)(2,1)S(1)} async-done(((bf16[6,4,8,8,256]{4,2,1,0,3:T(8,128)(2,1)}), bf16[6,4,8,8,256]{4,2,1,0,3:T(8,128)(2,1)S(1)}, u32[]{:S(2)}, u32[]{:S(2)}) %all-to-all-start.1) | async-done | bytes 786464 | tf_op jit(solution)/shard_map/all_to_all | solution.py:52
  63.8 3.5 %all-to-all-start = ((bf16[6,4,8,8,256]{4,2,1,0,3:T(8,128)(2,1)}), bf16[6,4,8,8,256]{4,2,1,0,3:T(8,128)(2,1)S(1)}, u32[]{:S(2)}, u32[]{:S(2)}) async-start(bf16[6,4,8,8,256]{4,2,1,0,3:T(8,128)(2,1)} %bitcast.73), calls=%async_computation | async-start | bytes 1572864 | tf_op jit(solution)/shard_map/all_to_all | solution.py:51
  68.0 35.4 %all_gather.6 = bf16[256,256]{1,0:T(8,128)(2,1)S(1)} all-gather(bf16[8,256]{1,0:T(8,128)(2,1)S(1)} %copy-done.4), channel_id=1, replica_groups=mesh['tm'=32,'height'=8,'rep'=2] {'tm'}, dimensions={0}, use_global_device_ids=true | all-gather | bytes 135168 | tf_op jit(solution)/shard_map/all_gather | solution.py:71
  103.5 31.1 %all_gather.7 = bf16[256,256]{1,0:T(8,128)(2,1)S(1)} all-gather(bf16[8,256]{1,0:T(8,128)(2,1)S(1)} %copy-done.5), channel_id=1, replica_groups=mesh['tm'=32,'height'=8,'rep'=2] {'tm'}, dimensions={0}, use_global_device_ids=true | all-gather | bytes 135168 | tf_op jit(solution)/shard_map/all_gather | solution.py:72
  135.4 3.4 %collective-permute-start.2 = (bf16[6,32,8,256]{3,2,1,0:T(8,128)(2,1)S(1)}, bf16[6,32,8,256]{3,2,1,0:T(8,128)(2,1)}, u32[]{:S(2)}, u32[]{:S(2)}) collective-permute-start(bf16[6,32,8,256]{3,2,1,0:T(8,128)(2,1)S(1)} %bitcast.104), channel_id=1, source_target_pairs={{0,16},{16,32},{32,48},{48,64},{64,80},{80,96},{96,112},{112,128},... | collective-permute-start | bytes 2359304 | tf_op jit(solution)/shard_map/ppermute | solution.py:13
  138.7 1.9 collective-permute-start.3
  140.7 3.6 %collective-permute-start = (bf16[6,32,8,256]{3,2,1,0:T(8,128)(2,1)S(1)}, bf16[6,32,8,256]{3,2,1,0:T(8,128)(2,1)}, u32[]{:S(2)}, u32[]{:S(2)}) collective-permute-start(bf16[6,32,8,256]{3,2,1,0:T(8,128)(2,1)S(1)} %bitcast.107), channel_id=1, source_target_pairs={{0,16},{16,32},{32,48},{48,64},{64,80},{80,96},{96,112},{112,128},... | collective-permute-start | bytes 2359304 | tf_op jit(solution)/shard_map/ppermute | solution.py:13
  144.4 1.9 collective-permute-start.1
  147.7 2.9 fusion.37
  150.7 2.7 fusion.38
  153.4 3.2 %select_maximum_fusion = bf16[18,48,8,256]{3,2,1,0:T(8,128)(2,1)} fusion(bf16[6,32,8,256]{3,2,1,0:T(8,128)(2,1)} %collective-permute-done.3, bf16[6,32,8,256]{3,2,1,0:T(8,128)(2,1)S(1)} %bitcast.106, bf16[6,32,8,256]{3,2,1,0:T(8,128)(2,1)} %collective-permute-done.2), kind=kLoop, calls=%fused_computation.40 | loop fusion | flops 21233664 | bytes 5898240 | tf_op jit(solution)/shard_map/concatenate | solution.py:62
  156.6 4.0 %collective-permute-done.1 = bf16[6,32,8,256]{3,2,1,0:T(8,128)(2,1)} collective-permute-done((bf16[6,32,8,256]{3,2,1,0:T(8,128)(2,1)S(1)}, bf16[6,32,8,256]{3,2,1,0:T(8,128)(2,1)}, u32[]{:S(2)}, u32[]{:S(2)}) %collective-permute-start.1) | collective-permute-done | bytes 786464 | tf_op jit(solution)/shard_map/ppermute | solution.py:13
  160.6 3.3 %select_maximum_fusion.2 = bf16[18,48,8,256]{3,2,1,0:T(8,128)(2,1)} fusion(bf16[6,32,8,256]{3,2,1,0:T(8,128)(2,1)} %collective-permute-done.1, bf16[6,32,8,256]{3,2,1,0:T(8,128)(2,1)S(1)} %bitcast.109, bf16[6,32,8,256]{3,2,1,0:T(8,128)(2,1)} %collective-permute-done), kind=kLoop, calls=%fused_computation.42 | loop fusion | flops 21233664 | bytes 5898240 | tf_op jit(solution)/shard_map/concatenate | solution.py:61
  164.4 113.0 %while.35 = (s32[]{:T(128)}, bf16[4,6,8,8,256]{4,3,2,0,1:T(8,128)(2,1)}, s32[4]{0:T(128)}, f32[2,6,32,8]{3,2,1,0:T(8,128)}, f32[2,6,32,8]{3,2,1,0:T(8,128)}, /*i...) while((s32[]{:T(128)}, ...), condition=%wide.region_7.8_spmd.clone, body=%wide.region_2.7_spmd.clone.sunk | while | flops 688964800 | bytes 29171604 | solution.py:138
  167.3 2.3 constant_dynamic-slice_fusion.15
  169.6 1.8 constant_dynamic-slice_fusion.12
  171.4 1.6 constant_dynamic-slice_fusion.14
  176.0 14.6 %while.36 = (s32[]{:T(128)}, bf16[2,384,128]{2,1,0:T(8,128)(2,1)}, f32[2,384,128]{2,1,0:T(8,128)}, f32[2,384]{1,0:T(2,128)S(1)}, s32[2]{0:T(128)S(1)}, /*index=5...) while((s32[]{:T(128)}, bf16[2,384,128]{2,1,0:T(8,128)(2,1)}, ...), condition=%wide.region_6.6_spmd.clone, body=%wide.region_3.5_spmd.clone.sunk | while | flops 688964352 | bytes 19708300 | solution.py:133
  178.9 1.9 fusion.58
  186.2 1.9 fusion.58
  189.1 1.6 fusion.61
  195.6 2.3 constant_dynamic-slice_fusion.15
  197.8 1.8 constant_dynamic-slice_fusion.12
  199.6 1.6 constant_dynamic-slice_fusion.14
  204.2 14.7 %while.36 = (s32[]{:T(128)}, bf16[2,384,128]{2,1,0:T(8,128)(2,1)}, f32[2,384,128]{2,1,0:T(8,128)}, f32[2,384]{1,0:T(2,128)S(1)}, s32[2]{0:T(128)S(1)}, /*index=5...) while((s32[]{:T(128)}, bf16[2,384,128]{2,1,0:T(8,128)(2,1)}, ...), condition=%wide.region_6.6_spmd.clone, body=%wide.region_3.5_spmd.clone.sunk | while | flops 688964352 | bytes 19708300 | solution.py:133
  207.1 1.9 fusion.58
  210.0 1.6 fusion.61
  214.4 1.9 fusion.58
  223.8 2.3 constant_dynamic-slice_fusion.15
  226.1 1.8 constant_dynamic-slice_fusion.12
  227.8 1.6 constant_dynamic-slice_fusion.14
  232.5 14.7 %while.36 = (s32[]{:T(128)}, bf16[2,384,128]{2,1,0:T(8,128)(2,1)}, f32[2,384,128]{2,1,0:T(8,128)}, f32[2,384]{1,0:T(2,128)S(1)}, s32[2]{0:T(128)S(1)}, /*index=5...) while((s32[]{:T(128)}, bf16[2,384,128]{2,1,0:T(8,128)(2,1)}, ...), condition=%wide.region_6.6_spmd.clone, body=%wide.region_3.5_spmd.clone.sunk | while | flops 688964352 | bytes 19708300 | solution.py:133
  235.3 1.9 fusion.58
  238.2 1.6 fusion.61
  242.7 1.9 fusion.58
  252.0 2.3 constant_dynamic-slice_fusion.15
  254.3 1.8 constant_dynamic-slice_fusion.12
  256.1 1.6 constant_dynamic-slice_fusion.14
  260.7 14.6 %while.36 = (s32[]{:T(128)}, bf16[2,384,128]{2,1,0:T(8,128)(2,1)}, f32[2,384,128]{2,1,0:T(8,128)}, f32[2,384]{1,0:T(2,128)S(1)}, s32[2]{0:T(128)S(1)}, /*index=5...) while((s32[]{:T(128)}, bf16[2,384,128]{2,1,0:T(8,128)(2,1)}, ...), condition=%wide.region_6.6_spmd.clone, body=%wide.region_3.5_spmd.clone.sunk | while | flops 688964352 | bytes 19708300 | solution.py:133
  263.6 1.9 fusion.58
  266.5 1.6 fusion.61
  270.9 1.9 fusion.58
  273.8 1.6 fusion.61
  278.5 25.8 %all_to_all.60 = bf16[6,32,8,1,256]{4,2,0,3,1:T(8,128)(2,1)S(1)} all-to-all(bf16[6,32,8,1,256]{4,2,0,3,1:T(8,128)(2,1)S(1)} %copy.68), channel_id=1, replica_groups=mesh['tm'=32,'height'=8,'rep'=2] {'height'}, dimensions={1} | all-to-all | bytes 1572864 | tf_op jit(solution)/shard_map/all_to_all | solution.py:142
  (198 shorter events, 64.8 us)
Async XLA Ops:
  0.0 13.1 %copy-start.2 = (bf16[6,4,8,2048]{3,2,1,0:T(8,128)(2,1)S(1)}, bf16[6,4,8,2048]{3,2,1,0:T(8,128)(2,1)}, u32[]{:S(2)}) copy-start(bf16[6,4,8,2048]{3,2,1,0:T(8,128)(2,1)} %param.11) | copy-start | bytes 2359300
  0.0 40.2 %copy-start.3 = (bf16[6,4,8,2048]{3,2,1,0:T(8,128)(2,1)S(1)}, bf16[6,4,8,2048]{3,2,1,0:T(8,128)(2,1)}, u32[]{:S(2)}) copy-start(bf16[6,4,8,2048]{3,2,1,0:T(8,128)(2,1)} %param.10) | copy-start | bytes 2359300
  2.2 34.4 %all-to-all-start.2 = ((bf16[6,4,8,8,256]{4,2,1,0,3:T(8,128)(2,1)}), bf16[6,4,8,8,256]{4,2,1,0,3:T(8,128)(2,1)S(1)}, u32[]{:S(2)}, u32[]{:S(2)}) async-start(bf16[6,4,8,8,256]{4,2,1,0,3:T(8,128)(2,1)} %bitcast.71), calls=%async_computation.2 | async-start | bytes 1572864 | tf_op jit(solution)/shard_map/all_to_all | solution.py:53
  13.1 54.9 %copy-start.4 = (bf16[8,256]{1,0:T(8,128)(2,1)S(1)}, bf16[8,256]{1,0:T(8,128)(2,1)}, u32[]{:S(2)}) copy-start(bf16[8,256]{1,0:T(8,128)(2,1)} %param.13) | copy-start | bytes 12292
  13.1 90.4 %copy-start.5 = (bf16[8,256]{1,0:T(8,128)(2,1)S(1)}, bf16[8,256]{1,0:T(8,128)(2,1)}, u32[]{:S(2)}) copy-start(bf16[8,256]{1,0:T(8,128)(2,1)} %param.14) | copy-start | bytes 12292
  36.7 27.1 %all-to-all-start.1 = ((bf16[6,4,8,8,256]{4,2,1,0,3:T(8,128)(2,1)}), bf16[6,4,8,8,256]{4,2,1,0,3:T(8,128)(2,1)S(1)}, u32[]{:S(2)}, u32[]{:S(2)}) async-start(bf16[6,4,8,8,256]{4,2,1,0,3:T(8,128)(2,1)} %bitcast.72), calls=%async_computation.1 | async-start | bytes 1572864 | tf_op jit(solution)/shard_map/all_to_all | solution.py:52
  63.8 82.5 %all-to-all-start = ((bf16[6,4,8,8,256]{4,2,1,0,3:T(8,128)(2,1)}), bf16[6,4,8,8,256]{4,2,1,0,3:T(8,128)(2,1)S(1)}, u32[]{:S(2)}, u32[]{:S(2)}) async-start(bf16[6,4,8,8,256]{4,2,1,0,3:T(8,128)(2,1)} %bitcast.73), calls=%async_computation | async-start | bytes 1572864 | tf_op jit(solution)/shard_map/all_to_all | solution.py:51
  135.4 18.0 %collective-permute-start.2 = (bf16[6,32,8,256]{3,2,1,0:T(8,128)(2,1)S(1)}, bf16[6,32,8,256]{3,2,1,0:T(8,128)(2,1)}, u32[]{:S(2)}, u32[]{:S(2)}) collective-permute-start(bf16[6,32,8,256]{3,2,1,0:T(8,128)(2,1)S(1)} %bitcast.104), channel_id=1, source_target_pairs={{0,16},{16,32},{32,48},{48,64},{64,80},{80,96},{96,112},{112,128},... | collective-permute-start | bytes 2359304 | tf_op jit(solution)/shard_map/ppermute | solution.py:13
  138.7 14.6 %collective-permute-start.3 = (bf16[6,32,8,256]{3,2,1,0:T(8,128)(2,1)S(1)}, bf16[6,32,8,256]{3,2,1,0:T(8,128)(2,1)}, u32[]{:S(2)}, u32[]{:S(2)}) collective-permute-start(bf16[6,32,8,256]{3,2,1,0:T(8,128)(2,1)S(1)} %bitcast.105), channel_id=1, source_target_pairs={{16,0},{32,16},{48,32},{64,48},{80,64},{96,80},{112,96},{128,112},... | collective-permute-start | bytes 2359304 | tf_op jit(solution)/shard_map/ppermute | solution.py:13
  140.7 15.8 %collective-permute-start = (bf16[6,32,8,256]{3,2,1,0:T(8,128)(2,1)S(1)}, bf16[6,32,8,256]{3,2,1,0:T(8,128)(2,1)}, u32[]{:S(2)}, u32[]{:S(2)}) collective-permute-start(bf16[6,32,8,256]{3,2,1,0:T(8,128)(2,1)S(1)} %bitcast.107), channel_id=1, source_target_pairs={{0,16},{16,32},{32,48},{48,64},{64,80},{80,96},{96,112},{112,128},... | collective-permute-start | bytes 2359304 | tf_op jit(solution)/shard_map/ppermute | solution.py:13
  144.4 16.2 %collective-permute-start.1 = (bf16[6,32,8,256]{3,2,1,0:T(8,128)(2,1)S(1)}, bf16[6,32,8,256]{3,2,1,0:T(8,128)(2,1)}, u32[]{:S(2)}, u32[]{:S(2)}) collective-permute-start(bf16[6,32,8,256]{3,2,1,0:T(8,128)(2,1)S(1)} %bitcast.108), channel_id=1, source_target_pairs={{16,0},{32,16},{48,32},{64,48},{80,64},{96,80},{112,96},{128,112},... | collective-permute-start | bytes 2359304 | tf_op jit(solution)/shard_map/ppermute | solution.py:13
  146.4 4.3 %copy-start.1 = (bf16[6,4,8,8,256]{4,2,1,3,0:T(8,128)(2,1)}, bf16[6,4,8,8,256]{4,2,1,3,0:T(8,128)(2,1)S(1)}, u32[]{:S(2)}) copy-start(bf16[6,4,8,8,256]{4,2,1,3,0:T(8,128)(2,1)S(1)} %copy.57) | copy-start | bytes 2359300
  176.0 1.2 copy-start.6
  180.8 1.0 copy-start
  181.8 1.6 copy-start.7
  183.3 1.2 copy-start.6
  188.1 1.0 copy-start
  189.1 1.6 copy-start.7
  204.2 1.2 copy-start.6
  209.0 1.0 copy-start
  210.0 1.6 copy-start.7
  211.6 1.2 copy-start.6
  216.3 1.0 copy-start
  217.3 1.6 copy-start.7
  232.5 1.2 copy-start.6
  237.2 1.0 copy-start
  238.2 1.6 copy-start.7
  239.8 1.2 copy-start.6
  244.6 1.0 copy-start
  245.6 1.6 copy-start.7
  260.7 1.2 copy-start.6
  265.5 1.0 copy-start
  266.5 1.6 copy-start.7
  268.0 1.2 copy-start.6
  272.8 1.0 copy-start
  273.8 1.6 copy-start.7
where the time goes:
time: 311 us; the launch traced here: 306 us
  blocking collectives  92.3 us (30%)
  local copies, waits for them, and re-layouts  73.2 us (24%)
  waiting for transfers between devices  49.1 us (16%)
  matrix products  31 us (10%)
  starting transfers between devices  28.8 us (9%)
  other arithmetic  20.3 us (7%)
  loops' own time  10.5 us (3%)
    all_gather x1, blocking collectives, per_device(): lax.all_gather(text_keys, 'tm', axis=0, tiled=True)  35.4 us
    all_gather x1, blocking collectives, per_device(): lax.all_gather(text_values, 'tm', axis=0, tiled=True)  31.1 us
    all_to_all x1, blocking collectives, per_device(): lax.all_to_all(attended_heads, 'height', split_axis=1, concat_axis=3, til...  25.8 us
    all_to_all x1, waiting for transfers between devices, per_device(): lax.all_to_all(to_heads(value_tokens), 'height', split_axis=3, concat_axi...  22.6 us
    all_to_all x1, waiting for transfers between devices, per_device(): lax.all_to_all(to_heads(key_tokens), 'height', split_axis=3, concat_axis=...  22.5 us
    dot_general x8, matrix products, one_head(): lax.dot_general(query_head, key_head, (((1,), (1,)), ((), ())), preferred...  15.1 us
    dot_general x8, matrix products, one_head(): jnp.dot(weights.astype(jnp.bfloat16), value_head, preferred_element_type=...  12.4 us
    all_to_all x1, starting transfers between devices, per_device(): lax.all_to_all(to_heads(value_tokens), 'height', split_axis=3, concat_axi...  10.9 us
  transfers between devices with their start and end apart: 7, of which 3 were waited for; matrix products, arithmetic and copies ran while one was open for 4% of the time, Pallas kernels for 0%

commit v1 on v0

v1 whole, which is shorter than its diff:
```python
import functools
import math

import jax
import jax.numpy as jnp
from jax import lax
from jax.experimental import pallas as pl
from jax.experimental.pallas import tpu as pltpu
from jax.sharding import PartitionSpec as P

DH = 128
ZT = 2
LOG2E = 1.4426950408889634


def kernel(
    peers,
    frames_axis,
    heads,
    cells,
    text_rows,
    q_ref,
    k_ref,
    v_ref,
    tk_ref,
    tv_ref,
    len_ref,
    out_ref,
    kv,
    qh,
    oh,
    text,
    text_k,
    text_v,
    a2a_send,
    a2a_recv,
    halo_send,
    halo_recv,
    out_send,
    out_recv,
    text_send,
    text_recv,
    local_sem,
):
    me_t = lax.axis_index("tm")
    me_z = lax.axis_index("height")
    tiles = peers // ZT
    nxt = lax.rem(me_t + 1, frames_axis)
    prv = lax.rem(me_t + frames_axis - 1, frames_axis)

    def offset(j):
        return jnp.where(lax.rem(j, 2) == 1, (j + 1) // 2, peers - j // 2)

    def columns(z, h):
        return pl.ds(pl.multiple_of((z * heads + h) * DH, DH), DH)

    barrier = pltpu.get_barrier_semaphore()

    def greet_z(j, c):
        pl.semaphore_signal(barrier, inc=1, device_id={"height": lax.rem(me_z + j, peers)})
        return c

    def greet_t(j, c):
        pl.semaphore_signal(barrier, inc=1, device_id={"tm": lax.rem(me_t + j, frames_axis)})
        return c

    lax.fori_loop(1, peers, greet_z, 0)
    lax.fori_loop(1, frames_axis, greet_t, 0)
    pl.semaphore_wait(barrier, peers - 1 + frames_axis - 1)

    sources = (k_ref, v_ref, q_ref)

    def landing(which, h, z):
        return qh.at[h, z] if which == 2 else kv.at[1, h, z, which]

    def a2a(which, h, d, z):
        return pltpu.make_async_remote_copy(
            src_ref=sources[which].at[:, columns(z, h)],
            dst_ref=landing(which, h, me_z),
            send_sem=a2a_send.at[h, which, d],
            recv_sem=a2a_recv.at[h, which, d],
            device_id={"height": z},
        )

    def arrival(which, h, d, z):
        return pltpu.make_async_remote_copy(
            src_ref=sources[which].at[:, columns(z, h)],
            dst_ref=landing(which, h, z),
            send_sem=a2a_send.at[h, which, d],
            recv_sem=a2a_recv.at[h, which, d],
            device_id={"height": z},
        )

    def own(which, h):
        return pltpu.make_async_copy(
            sources[which].at[:, columns(me_z, h)], landing(which, h, me_z), local_sem.at[h, which]
        )

    def send_all(which_list, h):
        def step(j, c):
            d = offset(j)
            z = lax.rem(me_z + d, peers)
            for which in which_list:
                a2a(which, h, d, z).start()
            return c

        lax.fori_loop(1, peers, step, 0)

    def halo(h, z, side):
        return pltpu.make_async_remote_copy(
            src_ref=kv.at[1, h, z],
            dst_ref=kv.at[2 * side, h, z],
            send_sem=halo_send.at[h, side, z],
            recv_sem=halo_recv.at[h, side, z],
            device_id={"tm": nxt if side == 0 else prv},
        )

    def forward(h):
        for which in range(2):
            own(which, h).wait()
        for side in range(2):
            halo(h, me_z, side).start()

        def step(j, c):
            d = offset(j)
            z = lax.rem(me_z + peers - d, peers)
            for which in range(2):
                arrival(which, h, d, z).wait_recv()
            for side in range(2):
                halo(h, z, side).start()
            return c

        lax.fori_loop(1, peers, step, 0)

    for h in range(heads):
        for which in range(3):
            own(which, h).start()
    send_all((0, 1), 0)

    text[me_t, :, : heads * DH] = tk_ref[...].astype(jnp.float32)
    text[me_t, :, heads * DH :] = tv_ref[...].astype(jnp.float32)

    def text_step(j, c):
        pltpu.make_async_remote_copy(
            src_ref=text.at[me_t],
            dst_ref=text.at[me_t],
            send_sem=text_send,
            recv_sem=text_recv,
            device_id={"tm": lax.rem(me_t + j, frames_axis)},
        ).start()
        return c

    lax.fori_loop(1, frames_axis, text_step, 0)
    for h in range(1, heads):
        send_all((0, 1), h)
    forward(0)
    for h in range(heads):
        send_all((2,), h)
    for h in range(1, heads):
        forward(h)

    rest = text.at[pl.ds(1, frames_axis - 1)]
    all_text = pltpu.make_async_remote_copy(
        src_ref=rest, dst_ref=rest, send_sem=text_send, recv_sem=text_recv, device_id={"tm": nxt}
    )
    all_text.wait()
    for h in range(heads):
        lane = slice(h * DH, (h + 1) * DH)
        lane_v = slice((heads + h) * DH, (heads + h + 1) * DH)
        text_k[h] = text[:, :, lane].reshape(-1, DH).astype(jnp.bfloat16)
        text_v[h] = text[:, :, lane_v].reshape(-1, DH).astype(jnp.bfloat16)

    scale = LOG2E / math.sqrt(DH)
    first = jnp.where(me_t == 0, 1, 0)
    last = jnp.where(me_t == frames_axis - 1, 2, 3)

    def scores_of(q, k):
        s = lax.dot_general(q, k, (((1,), (1,)), ((), ())), preferred_element_type=jnp.float32)
        return s * scale

    def tile(h, a, start, count):
        rows = ZT * cells
        q = qh[h, pl.ds(ZT * a, ZT)].reshape(rows, DH)
        s = scores_of(q, text_k[h])
        place = lax.broadcasted_iota(jnp.int32, s.shape, 1)
        s = jnp.where(place < len_ref[0], s, -jnp.inf)
        top = jnp.max(s, 1, keepdims=True)
        p = jnp.exp2(s - top)
        total = jnp.sum(p, 1, keepdims=True)
        acc = jnp.dot(p.astype(jnp.bfloat16), text_v[h], preferred_element_type=jnp.float32)

        def window(t, carry):
            top, total, acc = carry
            k = kv[t, h, pl.ds(start, count), 0].reshape(count * cells, DH)
            v = kv[t, h, pl.ds(start, count), 1].reshape(count * cells, DH)
            s = scores_of(q, k)
            new = jnp.maximum(top, jnp.max(s, 1, keepdims=True))
            fade = jnp.exp2(top - new)
            p = jnp.exp2(s - new)
            total = total * fade + jnp.sum(p, 1, keepdims=True)
            acc = acc * fade + jnp.dot(
                p.astype(jnp.bfloat16), v, preferred_element_type=jnp.float32
            )
            return new, total, acc

        top, total, acc = lax.fori_loop(first, last, window, (top, total, acc))
        oh[h, pl.ds(ZT * a, ZT)] = (
            (acc / total).astype(jnp.bfloat16).reshape(ZT, cells, DH)
        )

    def result(h, z):
        return pltpu.make_async_remote_copy(
            src_ref=oh.at[h, z],
            dst_ref=out_ref.at[:, columns(me_z, h)],
            send_sem=out_send.at[h, z],
            recv_sem=out_recv.at[h, me_z],
            device_id={"height": z},
        )

    def result_own(h):
        return pltpu.make_async_copy(
            oh.at[h, me_z], out_ref.at[:, columns(me_z, h)], out_send.at[h, me_z]
        )

    def send_tile(h, a):
        for i in range(ZT):
            z = ZT * a + i

            @pl.when(z != me_z)
            def _():
                result(h, z).start()

            @pl.when(z == me_z)
            def _():
                result_own(h).start()

    for h in range(heads):
        own(2, h).wait()

        def q_step(j, c, h=h):
            d = offset(j)
            arrival(2, h, d, lax.rem(me_z + peers - d, peers)).wait_recv()
            return c

        lax.fori_loop(1, peers, q_step, 0)

        def halo_step(z, c, h=h):
            for side in range(2):
                halo(h, z, side).wait_recv()
            return c

        lax.fori_loop(0, peers, halo_step, 0)

        def edge(i, c, h=h):
            a = i * (tiles - 1)
            tile(h, a, a * ZT - i * ZT, 2 * ZT)
            send_tile(h, a)
            return c

        def inner(a, c, h=h):
            tile(h, a, (a - 1) * ZT, 3 * ZT)
            send_tile(h, a)
            return c

        lax.fori_loop(0, 2, edge, 0)
        lax.fori_loop(1, tiles - 1, inner, 0)

    for h in range(heads):
        result_own(h).wait()

        def end_step(j, c, h=h):
            d = offset(j)
            z = lax.rem(me_z + d, peers)
            for which in range(3):
                a2a(which, h, d, z).wait_send()
            result(h, z).wait_send()
            pltpu.make_async_remote_copy(
                src_ref=oh.at[h, z],
                dst_ref=out_ref.at[:, columns(z, h)],
                send_sem=out_send.at[h, z],
                recv_sem=out_recv.at[h, z],
                device_id={"height": z},
            ).wait_recv()
            return c

        lax.fori_loop(1, peers, end_step, 0)

        def halo_end(z, c, h=h):
            for side in range(2):
                halo(h, z, side).wait_send()
            return c

        lax.fori_loop(0, peers, halo_end, 0)


def per_device(queries, key_tokens, value_tokens, text_keys, text_values, text_length):
    shape = queries.shape
    features = shape[3]
    cells = shape[0] * shape[1] * shape[2]
    peers = lax.axis_size("height")
    frames_axis = lax.axis_size("tm")
    heads = features // DH // peers
    text_rows = text_keys.shape[0]
    flat = [x.reshape(cells, features) for x in (queries, key_tokens, value_tokens)]
    any_space = pl.BlockSpec(memory_space=pl.ANY)
    vmem = pl.BlockSpec(memory_space=pltpu.VMEM)
    dma = pltpu.SemaphoreType.DMA
    result = pl.pallas_call(
        functools.partial(kernel, peers, frames_axis, heads, cells, text_rows),
        out_shape=jax.ShapeDtypeStruct((cells, features), jnp.bfloat16),
        in_specs=[any_space] * 3 + [vmem] * 2 + [pl.BlockSpec(memory_space=pltpu.SMEM)],
        out_specs=any_space,
        scratch_shapes=[
            pltpu.VMEM((3, heads, peers, 2, cells, DH), jnp.bfloat16),
            pltpu.VMEM((heads, peers, cells, DH), jnp.bfloat16),
            pltpu.VMEM((heads, peers, cells, DH), jnp.bfloat16),
            pltpu.VMEM((frames_axis, text_rows, 2 * heads * DH), jnp.float32),
            pltpu.VMEM((heads, frames_axis * text_rows, DH), jnp.bfloat16),
            pltpu.VMEM((heads, frames_axis * text_rows, DH), jnp.bfloat16),
            dma((heads, 3, peers)),
            dma((heads, 3, peers)),
            dma((heads, 2, peers)),
            dma((heads, 2, peers)),
            dma((heads, peers)),
            dma((heads, peers)),
            dma,
            dma,
            dma((heads, 3)),
        ],
        compiler_params=pltpu.CompilerParams(
            collective_id=0, has_side_effects=True, vmem_limit_bytes=62 * 1024 * 1024
        ),
        cost_estimate=pl.CostEstimate(
            flops=5_000_000_000, bytes_accessed=4_000_000, transcendentals=10_000_000
        ),
    )(*flat, text_keys, text_values, text_length)
    return result.reshape(shape)


def solution(mesh):
    placed = (
        P(("rep", "tm"), "height", None, None),
        P(("rep", "tm"), "height", None, None),
        P(("rep", "tm"), "height", None, None),
        P(("rep", "tm"), "height"),
        P(("rep", "tm"), "height"),
        P("rep"),
    )
    return jax.shard_map(
        per_device,
        mesh=mesh,
        in_specs=placed,
        out_specs=P(("rep", "tm"), "height", None, None),
        check_vma=False,
    )
```

time: 311 us -> 98.5 us (0.32)
  Pallas kernels: 0 us -> 93.9 us
  blocking collectives: 92.3 us -> 0 us
  local copies, waits for them, and re-layouts: 73.2 us -> 2.09 us
  waiting for transfers between devices: 49.1 us -> 0 us
  matrix products: 31 us -> 0 us
  starting transfers between devices: 28.8 us -> 0 us
  other arithmetic: 20.3 us -> 0 us
  loops' own time: 10.5 us -> 0 us
    pallas_call x0 -> x1, Pallas kernels: none -> 93.9 us  [per_device(): pl.pallas_call(functools.partial(kernel, peers, frames_axis, heads, cells...]
    all_gather x2 -> x0, blocking collectives: 66.5 us -> none  [the longest x1 35.4 us: per_device(): lax.all_gather(text_keys, 'tm', axis=0, tiled=True)]
    all_to_all x3 -> x0, waiting for transfers between devices: 45.1 us -> none  [the longest x1 22.6 us: per_device(): lax.all_to_all(to_heads(value_tokens), 'height', split_axis=3, concat_axi...]
    dynamic_slice x36 -> x0, local copies, waits for them, and re-layouts: 35.8 us -> none  [the longest x4 9.01 us: one_tile(): lax.dynamic_slice(values_window, starts, (3 * frames, 3 * TH, columns, gr...]
    dot_general x18 -> x0, matrix products: 31 us -> none  [the longest x8 15.1 us: one_head(): lax.dot_general(query_head, key_head, (((1,), (1,)), ((), ())), preferred...]
    all_to_all x1 -> x0, blocking collectives: 25.8 us -> none  [per_device(): lax.all_to_all(attended_heads, 'height', split_axis=1, concat_axis=3, til...]
    all_to_all x3 -> x0, starting transfers between devices: 18 us -> none  [the longest x1 10.9 us: per_device(): lax.all_to_all(to_heads(value_tokens), 'height', split_axis=3, concat_axi...]
    broadcast_in_dim x20 -> x0, local copies, waits for them, and re-layouts: 11.5 us -> none  [the longest x8 7.77 us: one_head(): scores = jnp.where(valid_keys[None, :], scores, -jnp.inf)]
  transfers between devices with their start and end apart: 7 -> 0, of which waited for: 3 -> 0; matrix products, arithmetic and copies ran while one was open for 4% -> 0% of each run, Pallas kernels for 0% -> 0%
where the time goes in v1:
time: 98.5 us; the launch traced here: 96.6 us
  Pallas kernels  93.9 us (95%)
  local copies, waits for them, and re-layouts  2.09 us (2%)
    pallas_call x1, Pallas kernels, per_device(): pl.pallas_call(functools.partial(kernel, peers, frames_axis, heads, cells...  93.9 us
    unnamed x1, local copies, waits for them, and re-layouts  2.09 us

profile of v1, /device:TPU:1, one launch (start us, length us, event | category | flops | bytes accessed | tf_op | source)
XLA Modules:
  0.0 96.6 jit_solution(17641490474306320489)
XLA Ops:
  0.7 93.9 %shard_map.64 = bf16[192,2048]{1,0:T(8,128)(2,1)} custom-call(bf16[192,2048]{1,0:T(8,128)(2,1)} %bitcast.5, bf16[192,2048]{1,0:T(8,128)(2,1)} %bitcast.6, bf16[192,2048]{1,0:T(8,128)(2,1)} %bitcast.7, bf16[8,256]{1,0:T(8,128)(2,1)} %tk_ref.1, bf16[8,256]{1,0:T(8,128)(2,1)} %tv_ref.1, s32[1]{0:T(128)S(6)} %copy.8.len_ref), custom_call_target="tpu_custom_call" | custom-call | flops 5000000000 | bytes 4000000 | tf_op jit(solution)/shard_map/pallas_call | solution.py:308
  94.5 2.1 %copy.9 = bf16[6,4,8,2048]{3,2,1,0:T(8,128)(2,1)} copy(bf16[6,4,8,2048]{3,2,1,0:T(8,128)(2,1)} %bitcast.4) | data formatting | bytes 1572864

commit v2 on v1

--- a/solution.py
+++ b/solution.py
@@ -32,6 +32,9 @@
     text,
     text_k,
     text_v,
+    text_s,
+    scores,
+    weights,
     a2a_send,
     a2a_recv,
     halo_send,
@@ -151,14 +154,11 @@
         return c
 
     lax.fori_loop(1, frames_axis, text_step, 0)
+    send_all((2,), 0)
+    forward(0)
+
     for h in range(1, heads):
         send_all((0, 1), h)
-    forward(0)
-    for h in range(heads):
-        send_all((2,), h)
-    for h in range(1, heads):
-        forward(h)
-
     rest = text.at[pl.ds(1, frames_axis - 1)]
     all_text = pltpu.make_async_remote_copy(
         src_ref=rest, dst_ref=rest, send_sem=text_send, recv_sem=text_recv, device_id={"tm": nxt}
@@ -171,41 +171,65 @@
         text_v[h] = text[:, :, lane_v].reshape(-1, DH).astype(jnp.bfloat16)
 
     scale = LOG2E / math.sqrt(DH)
-    first = jnp.where(me_t == 0, 1, 0)
-    last = jnp.where(me_t == frames_axis - 1, 2, 3)
-
-    def scores_of(q, k):
-        s = lax.dot_general(q, k, (((1,), (1,)), ((), ())), preferred_element_type=jnp.float32)
-        return s * scale
+    rows = ZT * cells
+    bias = (
+        jnp.where(me_t == 0, -jnp.inf, 0.0).astype(jnp.float32),
+        jnp.float32(0.0),
+        jnp.where(me_t == frames_axis - 1, -jnp.inf, 0.0).astype(jnp.float32),
+    )
+    ones = jnp.ones((3 * ZT * cells, DH), jnp.bfloat16)
+
+    def product(q, k):
+        return lax.dot_general(q, k, (((1,), (1,)), ((), ())), preferred_element_type=jnp.float32)
+
+    def lanes_max(s):
+        parts = [s[:, i : i + DH] for i in range(0, s.shape[1], DH)]
+        return functools.reduce(jnp.maximum, parts)
+
+    def weights_of(s, shift):
+        parts = [
+            jnp.exp2(s[:, i : i + DH] * scale - shift).astype(jnp.bfloat16)
+            for i in range(0, s.shape[1], DH)
+        ]
+        return jnp.concatenate(parts, 1)
 
     def tile(h, a, start, count):
-        rows = ZT * cells
+        n = count * cells
+        chunks = [(c, min(256, n - c)) for c in range(0, n, 256)]
         q = qh[h, pl.ds(ZT * a, ZT)].reshape(rows, DH)
-        s = scores_of(q, text_k[h])
+        s = product(q, text_k[h])
         place = lax.broadcasted_iota(jnp.int32, s.shape, 1)
         s = jnp.where(place < len_ref[0], s, -jnp.inf)
-        top = jnp.max(s, 1, keepdims=True)
-        p = jnp.exp2(s - top)
-        total = jnp.sum(p, 1, keepdims=True)
-        acc = jnp.dot(p.astype(jnp.bfloat16), text_v[h], preferred_element_type=jnp.float32)
-
-        def window(t, carry):
-            top, total, acc = carry
-            k = kv[t, h, pl.ds(start, count), 0].reshape(count * cells, DH)
-            v = kv[t, h, pl.ds(start, count), 1].reshape(count * cells, DH)
-            s = scores_of(q, k)
-            new = jnp.maximum(top, jnp.max(s, 1, keepdims=True))
-            fade = jnp.exp2(top - new)
-            p = jnp.exp2(s - new)
-            total = total * fade + jnp.sum(p, 1, keepdims=True)
-            acc = acc * fade + jnp.dot(
-                p.astype(jnp.bfloat16), v, preferred_element_type=jnp.float32
+        text_s[...] = s
+        top = lanes_max(s)
+        for t in range(3):
+            k = kv[t, h, pl.ds(start, count), 0].reshape(n, DH)
+            part = None
+            for c, w in chunks:
+                s = product(q, k[c : c + w])
+                scores[t, :, c : c + w] = s
+                m = lanes_max(s)
+                part = m if part is None else jnp.maximum(part, m)
+            top = jnp.maximum(top, part + bias[t])
+        top = jnp.broadcast_to(jnp.max(top, 1, keepdims=True) * scale, (rows, DH))
+
+        acc = jnp.dot(
+            weights_of(text_s[...], top),
+            jnp.concatenate([text_v[h], ones[: text_v.shape[1]]], 1),
+            preferred_element_type=jnp.float32,
+        )
+        for t in range(3):
+            shift = top - bias[t]
+            for c, w in chunks:
+                weights[t, :, c : c + w] = weights_of(scores[t, :, c : c + w], shift)
+            v = kv[t, h, pl.ds(start, count), 1].reshape(n, DH)
+            acc = acc + jnp.dot(
+                weights[t, :, :n],
+                jnp.concatenate([v, ones[:n]], 1),
+                preferred_element_type=jnp.float32,
             )
-            return new, total, acc
-
-        top, total, acc = lax.fori_loop(first, last, window, (top, total, acc))
         oh[h, pl.ds(ZT * a, ZT)] = (
-            (acc / total).astype(jnp.bfloat16).reshape(ZT, cells, DH)
+            (acc[:, :DH] / acc[:, DH:]).astype(jnp.bfloat16).reshape(ZT, cells, DH)
         )
 
     def result(h, z):
@@ -234,15 +258,21 @@
             def _():
                 result_own(h).start()
 
-    for h in range(heads):
-        own(2, h).wait()
-
-        def q_step(j, c, h=h):
+    def wait_queries(h):
+        def q_step(j, c):
             d = offset(j)
             arrival(2, h, d, lax.rem(me_z + peers - d, peers)).wait_recv()
             return c
 
+        own(2, h).wait()
         lax.fori_loop(1, peers, q_step, 0)
+
+    for h in range(heads):
+        if h > 0:
+            forward(h)
+        wait_queries(h)
+        if h + 1 < heads:
+            send_all((2,), h + 1)
 
         def halo_step(z, c, h=h):
             for side in range(2):
@@ -251,19 +281,25 @@
 
         lax.fori_loop(0, peers, halo_step, 0)
 
-        def edge(i, c, h=h):
-            a = i * (tiles - 1)
-            tile(h, a, a * ZT - i * ZT, 2 * ZT)
+        def tile_step(i, c, h=h):
+            side = 1 + 2 * lax.rem(me_t, 2)
+            ahead = jnp.where(i == 0, 2, jnp.where(i == 1, side, jnp.where(i == 2, 4 - side, 0)))
+            a = lax.rem(me_z // ZT + ahead, tiles)
+            low = a == 0
+            at_edge = jnp.logical_or(low, a == tiles - 1)
+
+            @pl.when(at_edge)
+            def _():
+                tile(h, a, jnp.where(low, 0, (tiles - 2) * ZT), 2 * ZT)
+
+            @pl.when(jnp.logical_not(at_edge))
+            def _():
+                tile(h, a, (a - 1) * ZT, 3 * ZT)
+
             send_tile(h, a)
             return c
 
-        def inner(a, c, h=h):
-            tile(h, a, (a - 1) * ZT, 3 * ZT)
-            send_tile(h, a)
-            return c
-
-        lax.fori_loop(0, 2, edge, 0)
-        lax.fori_loop(1, tiles - 1, inner, 0)
+        lax.fori_loop(0, tiles, tile_step, 0)
 
     for h in range(heads):
         result_own(h).wait()
@@ -317,6 +353,9 @@
             pltpu.VMEM((frames_axis, text_rows, 2 * heads * DH), jnp.float32),
             pltpu.VMEM((heads, frames_axis * text_rows, DH), jnp.bfloat16),
             pltpu.VMEM((heads, frames_axis * text_rows, DH), jnp.bfloat16),
+            pltpu.VMEM((ZT * cells, frames_axis * text_rows), jnp.float32),
+            pltpu.VMEM((3, ZT * cells, 3 * ZT * cells), jnp.float32),
+            pltpu.VMEM((3, ZT * cells, 3 * ZT * cells), jnp.bfloat16),
             dma((heads, 3, peers)),
             dma((heads, 3, peers)),
             dma((heads, 2, peers)),

time: 98.5 us -> 91.9 us (0.933)
  Pallas kernels: 93.9 us -> 87.4 us
    pallas_call x1, Pallas kernels: 93.9 us -> 87.4 us  [per_device(): pl.pallas_call(functools.partial(kernel, peers, frames_axis, heads, cells...]
where the time goes in v2:
time: 91.9 us; the launch traced here: 90.2 us
  Pallas kernels  87.4 us (95%)
  local copies, waits for them, and re-layouts  2.09 us (2%)
    pallas_call x1, Pallas kernels, per_device(): pl.pallas_call(functools.partial(kernel, peers, frames_axis, heads, cells...  87.4 us
    unnamed x1, local copies, waits for them, and re-layouts  2.09 us

profile of v2, /device:TPU:1, one launch (start us, length us, event | category | flops | bytes accessed | tf_op | source)
XLA Modules:
  0.0 90.2 jit_solution(4957851066778432925)
XLA Ops:
  0.7 87.4 %shard_map.64 = bf16[192,2048]{1,0:T(8,128)(2,1)} custom-call(bf16[192,2048]{1,0:T(8,128)(2,1)} %bitcast.5, bf16[192,2048]{1,0:T(8,128)(2,1)} %bitcast.6, bf16[192,2048]{1,0:T(8,128)(2,1)} %bitcast.7, bf16[8,256]{1,0:T(8,128)(2,1)} %tk_ref.1, bf16[8,256]{1,0:T(8,128)(2,1)} %tv_ref.1, s32[1]{0:T(128)S(6)} %copy.8.len_ref), custom_call_target="tpu_custom_call" | custom-call | flops 5000000000 | bytes 4000000 | tf_op jit(solution)/shard_map/pallas_call | solution.py:344
  88.1 2.1 %copy.9 = bf16[6,4,8,2048]{3,2,1,0:T(8,128)(2,1)} copy(bf16[6,4,8,2048]{3,2,1,0:T(8,128)(2,1)} %bitcast.4) | data formatting | bytes 1572864

commit v3 on v2

--- a/solution.py
+++ b/solution.py
@@ -29,6 +29,7 @@
     kv,
     qh,
     oh,
+    relay,
     text,
     text_k,
     text_v,
@@ -41,6 +42,9 @@
     halo_recv,
     out_send,
     out_recv,
+    hop_send,
+    hop_recv,
+    pass_send,
     text_send,
     text_recv,
     local_sem,
@@ -99,15 +103,63 @@
             sources[which].at[:, columns(me_z, h)], landing(which, h, me_z), local_sem.at[h, which]
         )
 
-    def send_all(which_list, h):
+    opposite = lax.rem(me_z + peers // 2, peers)
+
+    def half(side):
+        return pl.ds(side * (cells // 2), cells // 2)
+
+    def shifted(by):
+        return lax.rem(me_z + peers + by, peers)
+
+    def hop(which, h, side):
+        if which == 3:
+            source = oh.at[h, opposite, half(side)]
+        else:
+            source = sources[which].at[half(side), columns(opposite, h)]
+        return pltpu.make_async_remote_copy(
+            src_ref=source,
+            dst_ref=relay.at[h, which, side],
+            send_sem=hop_send.at[h, which, side],
+            recv_sem=hop_recv.at[h, which, side],
+            device_id={"height": shifted(1 - 2 * side)},
+        )
+
+    def pass_on(which, h, side):
+        origin = shifted(2 * side - 1)
+        if which == 3:
+            target, counted = out_ref.at[half(side), columns(origin, h)], out_recv.at[h, origin]
+        else:
+            counted = a2a_recv.at[h, which, peers // 2]
+            if which == 2:
+                target = qh.at[h, origin, half(side)]
+            else:
+                target = kv.at[1, h, origin, which, half(side)]
+        return pltpu.make_async_remote_copy(
+            src_ref=relay.at[h, which, side],
+            dst_ref=target,
+            send_sem=pass_send.at[h, which, side],
+            recv_sem=counted,
+            device_id={"height": shifted((1 - 2 * side) * (peers // 2 - 1))},
+        )
+
+    def relay_step(which, h):
+        for side in range(2):
+            hop(which, h, side).wait_recv()
+            pass_on(which, h, side).start()
+
+    def send_all(which_list, h, farthest_first=False):
+        for which in which_list:
+            for side in range(2):
+                hop(which, h, side).start()
+
         def step(j, c):
-            d = offset(j)
+            d = offset(peers - 1 - j if farthest_first else j)
             z = lax.rem(me_z + d, peers)
             for which in which_list:
                 a2a(which, h, d, z).start()
             return c
 
-        lax.fori_loop(1, peers, step, 0)
+        lax.fori_loop(1, peers - 1, step, 0)
 
     def halo(h, z, side):
         return pltpu.make_async_remote_copy(
@@ -123,6 +175,8 @@
             own(which, h).wait()
         for side in range(2):
             halo(h, me_z, side).start()
+        for which in range(2):
+            relay_step(which, h)
 
         def step(j, c):
             d = offset(j)
@@ -154,7 +208,7 @@
         return c
 
     lax.fori_loop(1, frames_axis, text_step, 0)
-    send_all((2,), 0)
+    send_all((2,), 0, True)
     forward(0)
 
     for h in range(1, heads):
@@ -241,6 +295,15 @@
             device_id={"height": z},
         )
 
+    def result_arrival(h, z):
+        return pltpu.make_async_remote_copy(
+            src_ref=oh.at[h, z],
+            dst_ref=out_ref.at[:, columns(z, h)],
+            send_sem=out_send.at[h, z],
+            recv_sem=out_recv.at[h, z],
+            device_id={"height": z},
+        )
+
     def result_own(h):
         return pltpu.make_async_copy(
             oh.at[h, me_z], out_ref.at[:, columns(me_z, h)], out_send.at[h, me_z]
@@ -250,29 +313,37 @@
         for i in range(ZT):
             z = ZT * a + i
 
+            @pl.when(jnp.logical_and(z != me_z, z != opposite))
+            def _():
+                result(h, z).start()
+
+            @pl.when(z == opposite)
+            def _():
+                for side in range(2):
+                    hop(3, h, side).start()
+
+            @pl.when(z == me_z)
+            def _():
+                result_own(h).start()
+
+    def wait_queries(h, a):
+        for i in range(ZT):
+            z = ZT * a + i
+
             @pl.when(z != me_z)
             def _():
-                result(h, z).start()
+                arrival(2, h, lax.rem(me_z + peers - z, peers), z).wait_recv()
 
             @pl.when(z == me_z)
             def _():
-                result_own(h).start()
-
-    def wait_queries(h):
-        def q_step(j, c):
-            d = offset(j)
-            arrival(2, h, d, lax.rem(me_z + peers - d, peers)).wait_recv()
-            return c
-
-        own(2, h).wait()
-        lax.fori_loop(1, peers, q_step, 0)
+                own(2, h).wait()
 
     for h in range(heads):
         if h > 0:
             forward(h)
-        wait_queries(h)
         if h + 1 < heads:
-            send_all((2,), h + 1)
+            send_all((2,), h + 1, True)
+        relay_step(2, h)
 
         def halo_step(z, c, h=h):
             for side in range(2):
@@ -287,6 +358,11 @@
             a = lax.rem(me_z // ZT + ahead, tiles)
             low = a == 0
             at_edge = jnp.logical_or(low, a == tiles - 1)
+            wait_queries(h, a)
+
+            @pl.when(i == 2)
+            def _():
+                relay_step(3, h)
 
             @pl.when(at_edge)
             def _():
@@ -310,16 +386,15 @@
             for which in range(3):
                 a2a(which, h, d, z).wait_send()
             result(h, z).wait_send()
-            pltpu.make_async_remote_copy(
-                src_ref=oh.at[h, z],
-                dst_ref=out_ref.at[:, columns(z, h)],
-                send_sem=out_send.at[h, z],
-                recv_sem=out_recv.at[h, z],
-                device_id={"height": z},
-            ).wait_recv()
-            return c
-
-        lax.fori_loop(1, peers, end_step, 0)
+            result_arrival(h, z).wait_recv()
+            return c
+
+        lax.fori_loop(1, peers - 1, end_step, 0)
+        result_arrival(h, opposite).wait_recv()
+        for which in range(4):
+            for side in range(2):
+                hop(which, h, side).wait_send()
+                pass_on(which, h, side).wait_send()
 
         def halo_end(z, c, h=h):
             for side in range(2):
@@ -350,6 +425,7 @@
             pltpu.VMEM((3, heads, peers, 2, cells, DH), jnp.bfloat16),
             pltpu.VMEM((heads, peers, cells, DH), jnp.bfloat16),
             pltpu.VMEM((heads, peers, cells, DH), jnp.bfloat16),
+            pltpu.VMEM((heads, 4, 2, cells // 2, DH), jnp.bfloat16),
             pltpu.VMEM((frames_axis, text_rows, 2 * heads * DH), jnp.float32),
             pltpu.VMEM((heads, frames_axis * text_rows, DH), jnp.bfloat16),
             pltpu.VMEM((heads, frames_axis * text_rows, DH), jnp.bfloat16),
@@ -362,6 +438,9 @@
             dma((heads, 2, peers)),
             dma((heads, peers)),
             dma((heads, peers)),
+            dma((heads, 4, 2)),
+            dma((heads, 4, 2)),
+            dma((heads, 4, 2)),
             dma,
             dma,
             dma((heads, 3)),

time: 91.9 us -> 113 us (1.23); the launches traced: 90.2 us -> 113 us
  Pallas kernels: 87.4 us -> 110 us
    pallas_call x1, Pallas kernels: 87.4 us -> 110 us  [per_device(): pl.pallas_call(functools.partial(kernel, peers, frames_axis, heads, cells...]
where the time goes in v3:
time: 113 us
  Pallas kernels  110 us (97%)
  local copies, waits for them, and re-layouts  2.09 us (2%)
    pallas_call x1, Pallas kernels, per_device(): pl.pallas_call(functools.partial(kernel, peers, frames_axis, heads, cells...  110 us

profile of v3, /device:TPU:1, one launch (start us, length us, event | category | flops | bytes accessed | tf_op | source)
XLA Modules:
  0.0 112.6 jit_solution(15911852840752245770)
XLA Ops:
  0.7 109.9 %shard_map.64 = bf16[192,2048]{1,0:T(8,128)(2,1)} custom-call(bf16[192,2048]{1,0:T(8,128)(2,1)} %bitcast.5, bf16[192,2048]{1,0:T(8,128)(2,1)} %bitcast.6, bf16[192,2048]{1,0:T(8,128)(2,1)} %bitcast.7, bf16[8,256]{1,0:T(8,128)(2,1)} %tk_ref.1, bf16[8,256]{1,0:T(8,128)(2,1)} %tv_ref.1, s32[1]{0:T(128)S(6)} %copy.8.len_ref), custom_call_target="tpu_custom_call" | custom-call | flops 5000000000 | bytes 4000000 | tf_op jit(solution)/shard_map/pallas_call | solution.py:419
  110.5 2.1 %copy.9 = bf16[6,4,8,2048]{3,2,1,0:T(8,128)(2,1)} copy(bf16[6,4,8,2048]{3,2,1,0:T(8,128)(2,1)} %bitcast.4) | data formatting | bytes 1572864

commit v4 on v2

--- a/solution.py
+++ b/solution.py
@@ -99,12 +99,14 @@
             sources[which].at[:, columns(me_z, h)], landing(which, h, me_z), local_sem.at[h, which]
         )
 
+    def send(which_list, h, d):
+        z = lax.rem(me_z + d, peers)
+        for which in which_list:
+            a2a(which, h, d, z).start()
+
     def send_all(which_list, h):
         def step(j, c):
-            d = offset(j)
-            z = lax.rem(me_z + d, peers)
-            for which in which_list:
-                a2a(which, h, d, z).start()
+            send(which_list, h, offset(j))
             return c
 
         lax.fori_loop(1, peers, step, 0)
@@ -118,7 +120,7 @@
             device_id={"tm": nxt if side == 0 else prv},
         )
 
-    def forward(h):
+    def forward(h, beside):
         for which in range(2):
             own(which, h).wait()
         for side in range(2):
@@ -127,6 +129,7 @@
         def step(j, c):
             d = offset(j)
             z = lax.rem(me_z + peers - d, peers)
+            beside(j)
             for which in range(2):
                 arrival(which, h, d, z).wait_recv()
             for side in range(2):
@@ -135,15 +138,7 @@
 
         lax.fori_loop(1, peers, step, 0)
 
-    for h in range(heads):
-        for which in range(3):
-            own(which, h).start()
-    send_all((0, 1), 0)
-
-    text[me_t, :, : heads * DH] = tk_ref[...].astype(jnp.float32)
-    text[me_t, :, heads * DH :] = tv_ref[...].astype(jnp.float32)
-
-    def text_step(j, c):
+    def send_text(j):
         pltpu.make_async_remote_copy(
             src_ref=text.at[me_t],
             dst_ref=text.at[me_t],
@@ -151,24 +146,45 @@
             recv_sem=text_recv,
             device_id={"tm": lax.rem(me_t + j, frames_axis)},
         ).start()
+
+    share = -(-(frames_axis - 1) // (peers - 1))
+
+    def beside_first(j):
+        send((0, 1), 1, offset(j))
+
+        def step(i, c):
+            send_text(i)
+            return c
+
+        start = 1 + (j - 1) * share
+        lax.fori_loop(start, jnp.minimum(start + share, frames_axis), step, 0)
+
+    def beside_last(j):
+        send((2,), 0, offset(peers - j))
+
+    for h in range(heads):
+        for which in range(3):
+            own(which, h).start()
+    send_all((0, 1), 0)
+    own_text = [tk_ref[...].astype(jnp.float32), tv_ref[...].astype(jnp.float32)]
+    text[me_t] = jnp.concatenate(own_text, 0).astype(jnp.bfloat16)
+    forward(0, beside_first)
+    forward(1, beside_last)
+
+    def last_queries(j, c):
+        send((2,), 1, offset(peers - j))
         return c
 
-    lax.fori_loop(1, frames_axis, text_step, 0)
-    send_all((2,), 0)
-    forward(0)
-
-    for h in range(1, heads):
-        send_all((0, 1), h)
+    lax.fori_loop(1, peers, last_queries, 0)
     rest = text.at[pl.ds(1, frames_axis - 1)]
     all_text = pltpu.make_async_remote_copy(
         src_ref=rest, dst_ref=rest, send_sem=text_send, recv_sem=text_recv, device_id={"tm": nxt}
     )
     all_text.wait()
     for h in range(heads):
-        lane = slice(h * DH, (h + 1) * DH)
-        lane_v = slice((heads + h) * DH, (heads + h + 1) * DH)
-        text_k[h] = text[:, :, lane].reshape(-1, DH).astype(jnp.bfloat16)
-        text_v[h] = text[:, :, lane_v].reshape(-1, DH).astype(jnp.bfloat16)
+        both = text[:, :, h * DH : (h + 1) * DH].astype(jnp.float32)
+        text_k[h] = both[:, :text_rows].reshape(-1, DH).astype(jnp.bfloat16)
+        text_v[h] = both[:, text_rows:].reshape(-1, DH).astype(jnp.bfloat16)
 
     scale = LOG2E / math.sqrt(DH)
     rows = ZT * cells
@@ -258,22 +274,19 @@
             def _():
                 result_own(h).start()
 
-    def wait_queries(h):
-        def q_step(j, c):
-            d = offset(j)
-            arrival(2, h, d, lax.rem(me_z + peers - d, peers)).wait_recv()
-            return c
-
-        own(2, h).wait()
-        lax.fori_loop(1, peers, q_step, 0)
+    def wait_queries(h, a):
+        for i in range(ZT):
+            z = ZT * a + i
+
+            @pl.when(z != me_z)
+            def _():
+                arrival(2, h, lax.rem(me_z + peers - z, peers), z).wait_recv()
+
+            @pl.when(z == me_z)
+            def _():
+                own(2, h).wait()
 
     for h in range(heads):
-        if h > 0:
-            forward(h)
-        wait_queries(h)
-        if h + 1 < heads:
-            send_all((2,), h + 1)
-
         def halo_step(z, c, h=h):
             for side in range(2):
                 halo(h, z, side).wait_recv()
@@ -287,6 +300,7 @@
             a = lax.rem(me_z // ZT + ahead, tiles)
             low = a == 0
             at_edge = jnp.logical_or(low, a == tiles - 1)
+            wait_queries(h, a)
 
             @pl.when(at_edge)
             def _():
@@ -350,7 +364,7 @@
             pltpu.VMEM((3, heads, peers, 2, cells, DH), jnp.bfloat16),
             pltpu.VMEM((heads, peers, cells, DH), jnp.bfloat16),
             pltpu.VMEM((heads, peers, cells, DH), jnp.bfloat16),
-            pltpu.VMEM((frames_axis, text_rows, 2 * heads * DH), jnp.float32),
+            pltpu.VMEM((frames_axis, 2 * text_rows, heads * DH), jnp.bfloat16),
             pltpu.VMEM((heads, frames_axis * text_rows, DH), jnp.bfloat16),
             pltpu.VMEM((heads, frames_axis * text_rows, DH), jnp.bfloat16),
             pltpu.VMEM((ZT * cells, frames_axis * text_rows), jnp.float32),

time: 91.9 us -> 90.4 us (0.984); the launches traced: 90.2 us -> 90.2 us
  no operation moved by 1% of the time
where the time goes in v4:
time: 90.4 us; the launch traced here: 90.2 us
  Pallas kernels  87.4 us (97%)
  local copies, waits for them, and re-layouts  2.09 us (2%)
    pallas_call x1, Pallas kernels, per_device(): pl.pallas_call(functools.partial(kernel, peers, frames_axis, heads, cells...  87.4 us
    unnamed x1, local copies, waits for them, and re-layouts  2.09 us

profile of v4, /device:TPU:1, one launch (start us, length us, event | category | flops | bytes accessed | tf_op | source)
XLA Modules:
  0.0 90.2 jit_solution(465909683319123501)
XLA Ops:
  0.7 87.4 %shard_map.64 = bf16[192,2048]{1,0:T(8,128)(2,1)} custom-call(bf16[192,2048]{1,0:T(8,128)(2,1)} %bitcast.5, bf16[192,2048]{1,0:T(8,128)(2,1)} %bitcast.6, bf16[192,2048]{1,0:T(8,128)(2,1)} %bitcast.7, bf16[8,256]{1,0:T(8,128)(2,1)} %tk_ref.1, bf16[8,256]{1,0:T(8,128)(2,1)} %tv_ref.1, s32[1]{0:T(128)S(6)} %copy.8.len_ref), custom_call_target="tpu_custom_call" | custom-call | flops 5000000000 | bytes 4000000 | tf_op jit(solution)/shard_map/pallas_call | solution.py:358
  88.1 2.1 %copy.9 = bf16[6,4,8,2048]{3,2,1,0:T(8,128)(2,1)} copy(bf16[6,4,8,2048]{3,2,1,0:T(8,128)(2,1)} %bitcast.4) | data formatting | bytes 1572864

commit v5 on v4

--- a/solution.py
+++ b/solution.py
@@ -34,7 +34,6 @@
     text_v,
     text_s,
     scores,
-    weights,
     a2a_send,
     a2a_recv,
     halo_send,
@@ -120,12 +119,13 @@
             device_id={"tm": nxt if side == 0 else prv},
         )
 
-    def forward(h, beside):
+    def forward_own(h):
         for which in range(2):
             own(which, h).wait()
         for side in range(2):
             halo(h, me_z, side).start()
 
+    def forward(h, beside, first, end):
         def step(j, c):
             d = offset(j)
             z = lax.rem(me_z + peers - d, peers)
@@ -136,7 +136,7 @@
                 halo(h, z, side).start()
             return c
 
-        lax.fori_loop(1, peers, step, 0)
+        lax.fori_loop(first, end, step, 0)
 
     def send_text(j):
         pltpu.make_async_remote_copy(
@@ -160,7 +160,7 @@
         lax.fori_loop(start, jnp.minimum(start + share, frames_axis), step, 0)
 
     def beside_last(j):
-        send((2,), 0, offset(peers - j))
+        send((2,), 1, offset(peers - j))
 
     for h in range(heads):
         for which in range(3):
@@ -168,14 +168,16 @@
     send_all((0, 1), 0)
     own_text = [tk_ref[...].astype(jnp.float32), tv_ref[...].astype(jnp.float32)]
     text[me_t] = jnp.concatenate(own_text, 0).astype(jnp.bfloat16)
-    forward(0, beside_first)
-    forward(1, beside_last)
-
-    def last_queries(j, c):
-        send((2,), 1, offset(peers - j))
+
+    def first_queries(j, c):
+        send((2,), 0, offset(peers - j))
         return c
 
-    lax.fori_loop(1, peers, last_queries, 0)
+    lax.fori_loop(1, peers, first_queries, 0)
+    forward_own(0)
+    forward(0, beside_first, 1, peers)
+    forward_own(1)
+
     rest = text.at[pl.ds(1, frames_axis - 1)]
     all_text = pltpu.make_async_remote_copy(
         src_ref=rest, dst_ref=rest, send_sem=text_send, recv_sem=text_recv, device_id={"tm": nxt}
@@ -212,6 +214,7 @@
     def tile(h, a, start, count):
         n = count * cells
         chunks = [(c, min(256, n - c)) for c in range(0, n, 256)]
+        wide_chunks = [(0, 512), (512, n - 512)]
         q = qh[h, pl.ds(ZT * a, ZT)].reshape(rows, DH)
         s = product(q, text_k[h])
         place = lax.broadcasted_iota(jnp.int32, s.shape, 1)
@@ -229,21 +232,23 @@
             top = jnp.maximum(top, part + bias[t])
         top = jnp.broadcast_to(jnp.max(top, 1, keepdims=True) * scale, (rows, DH))
 
-        acc = jnp.dot(
-            weights_of(text_s[...], top),
-            jnp.concatenate([text_v[h], ones[: text_v.shape[1]]], 1),
-            preferred_element_type=jnp.float32,
-        )
-        for t in range(3):
-            shift = top - bias[t]
-            for c, w in chunks:
-                weights[t, :, c : c + w] = weights_of(scores[t, :, c : c + w], shift)
-            v = kv[t, h, pl.ds(start, count), 1].reshape(n, DH)
-            acc = acc + jnp.dot(
-                weights[t, :, :n],
-                jnp.concatenate([v, ones[:n]], 1),
-                preferred_element_type=jnp.float32,
-            )
+        pieces = [(t, c, w) for t in range(3) for c, w in wide_chunks]
+        values = [kv[t, h, pl.ds(start, count), 1].reshape(n, DH) for t in range(3)]
+        shifts = [top - b for b in bias]
+
+        def value_product(p, v):
+            both = jnp.concatenate([v, ones[: v.shape[0]]], 1)
+            return jnp.dot(p, both, preferred_element_type=jnp.float32)
+
+        acc = None
+        held = weights_of(text_s[...], top)
+        held_v = text_v[h]
+        for t, c, w in pieces:
+            p = weights_of(scores[t, :, c : c + w], shifts[t])
+            part = value_product(held, held_v)
+            acc = part if acc is None else acc + part
+            held, held_v = p, values[t][c : c + w]
+        acc = acc + value_product(held, held_v)
         oh[h, pl.ds(ZT * a, ZT)] = (
             (acc[:, :DH] / acc[:, DH:]).astype(jnp.bfloat16).reshape(ZT, cells, DH)
         )
@@ -311,6 +316,9 @@
                 tile(h, a, (a - 1) * ZT, 3 * ZT)
 
             send_tile(h, a)
+            if h == 0:
+                begin = 1 + 2 * i
+                forward(1, beside_last, begin, jnp.minimum(begin + 2, peers))
             return c
 
         lax.fori_loop(0, tiles, tile_step, 0)
@@ -369,7 +377,6 @@
             pltpu.VMEM((heads, frames_axis * text_rows, DH), jnp.bfloat16),
             pltpu.VMEM((ZT * cells, frames_axis * text_rows), jnp.float32),
             pltpu.VMEM((3, ZT * cells, 3 * ZT * cells), jnp.float32),
-            pltpu.VMEM((3, ZT * cells, 3 * ZT * cells), jnp.bfloat16),
             dma((heads, 3, peers)),
             dma((heads, 3, peers)),
             dma((heads, 2, peers)),

time: 90.4 us -> 93.6 us (1.035)
  Pallas kernels: 87.4 us -> 89.8 us
    pallas_call x1, Pallas kernels: 87.4 us -> 89.8 us  [per_device(): pl.pallas_call(functools.partial(kernel, peers, frames_axis, heads, cells...]
where the time goes in v5:
time: 93.6 us; the launch traced here: 92.5 us
  Pallas kernels  89.8 us (96%)
  local copies, waits for them, and re-layouts  2.09 us (2%)
    pallas_call x1, Pallas kernels, per_device(): pl.pallas_call(functools.partial(kernel, peers, frames_axis, heads, cells...  89.8 us
    unnamed x1, local copies, waits for them, and re-layouts  2.09 us

profile of v5, /device:TPU:1, one launch (start us, length us, event | category | flops | bytes accessed | tf_op | source)
XLA Modules:
  0.0 92.5 jit_solution(8231250705899043472)
XLA Ops:
  0.7 89.8 %shard_map.64 = bf16[192,2048]{1,0:T(8,128)(2,1)} custom-call(bf16[192,2048]{1,0:T(8,128)(2,1)} %bitcast.5, bf16[192,2048]{1,0:T(8,128)(2,1)} %bitcast.6, bf16[192,2048]{1,0:T(8,128)(2,1)} %bitcast.7, bf16[8,256]{1,0:T(8,128)(2,1)} %tk_ref.1, bf16[8,256]{1,0:T(8,128)(2,1)} %tv_ref.1, s32[1]{0:T(128)S(6)} %copy.8.len_ref), custom_call_target="tpu_custom_call" | custom-call | flops 5000000000 | bytes 4000000 | tf_op jit(solution)/shard_map/pallas_call | solution.py:366
  90.5 2.1 %copy.9 = bf16[6,4,8,2048]{3,2,1,0:T(8,128)(2,1)} copy(bf16[6,4,8,2048]{3,2,1,0:T(8,128)(2,1)} %bitcast.4) | data formatting | bytes 1572864

commit v6 on v3

--- a/solution.py
+++ b/solution.py
@@ -35,7 +35,6 @@
     text_v,
     text_s,
     scores,
-    weights,
     a2a_send,
     a2a_recv,
     halo_send,
@@ -55,8 +54,11 @@
     nxt = lax.rem(me_t + 1, frames_axis)
     prv = lax.rem(me_t + frames_axis - 1, frames_axis)
 
-    def offset(j):
-        return jnp.where(lax.rem(j, 2) == 1, (j + 1) // 2, peers - j // 2)
+    pairs = peers // 2 - 1
+
+    def offsets(p):
+        first = jnp.where(lax.rem(me_t, 2) == 0, p, peers - p)
+        return first, peers - first
 
     def columns(z, h):
         return pl.ds(pl.multiple_of((z * heads + h) * DH, DH), DH)
@@ -147,19 +149,15 @@
             hop(which, h, side).wait_recv()
             pass_on(which, h, side).start()
 
-    def send_all(which_list, h, farthest_first=False):
+    def start_hops(which_list, h):
         for which in which_list:
             for side in range(2):
                 hop(which, h, side).start()
 
-        def step(j, c):
-            d = offset(peers - 1 - j if farthest_first else j)
-            z = lax.rem(me_z + d, peers)
-            for which in which_list:
-                a2a(which, h, d, z).start()
-            return c
-
-        lax.fori_loop(1, peers - 1, step, 0)
+    def send_pair(which_list, h, p):
+        for which in which_list:
+            for d in offsets(p):
+                a2a(which, h, d, lax.rem(me_z + d, peers)).start()
 
     def halo(h, z, side):
         return pltpu.make_async_remote_copy(
@@ -170,34 +168,25 @@
             device_id={"tm": nxt if side == 0 else prv},
         )
 
-    def forward(h):
+    def forward_own(h):
         for which in range(2):
             own(which, h).wait()
         for side in range(2):
             halo(h, me_z, side).start()
+
+    def forward_from(h, d):
+        z = lax.rem(me_z + peers - d, peers)
         for which in range(2):
-            relay_step(which, h)
-
-        def step(j, c):
-            d = offset(j)
-            z = lax.rem(me_z + peers - d, peers)
-            for which in range(2):
-                arrival(which, h, d, z).wait_recv()
-            for side in range(2):
-                halo(h, z, side).start()
-            return c
-
-        lax.fori_loop(1, peers, step, 0)
-
-    for h in range(heads):
-        for which in range(3):
-            own(which, h).start()
-    send_all((0, 1), 0)
-
-    text[me_t, :, : heads * DH] = tk_ref[...].astype(jnp.float32)
-    text[me_t, :, heads * DH :] = tv_ref[...].astype(jnp.float32)
-
-    def text_step(j, c):
+            arrival(which, h, d, z).wait_recv()
+        for side in range(2):
+            halo(h, z, side).start()
+
+    def forward(h, beside, p):
+        beside(p)
+        for d in offsets(p):
+            forward_from(h, d)
+
+    def send_text(j):
         pltpu.make_async_remote_copy(
             src_ref=text.at[me_t],
             dst_ref=text.at[me_t],
@@ -205,24 +194,57 @@
             recv_sem=text_recv,
             device_id={"tm": lax.rem(me_t + j, frames_axis)},
         ).start()
+
+    share = -(-(frames_axis - 1) // pairs)
+
+    def beside_first(p):
+        send_pair((0, 1), 1, p)
+
+        def step(i, c):
+            send_text(i)
+            return c
+
+        start = 1 + (p - 1) * share
+        lax.fori_loop(start, jnp.minimum(start + share, frames_axis), step, 0)
+
+    def beside_last(p):
+        send_pair((2,), 1, pairs + 1 - p)
+
+    for h in range(heads):
+        for which in range(3):
+            own(which, h).start()
+    start_hops((0, 1, 2), 0)
+    for p in range(1, pairs):
+        send_pair((0, 1), 0, p)
+    own_text = [tk_ref[...].astype(jnp.float32), tv_ref[...].astype(jnp.float32)]
+    text[me_t] = jnp.concatenate(own_text, 0).astype(jnp.bfloat16)
+    for which in range(3):
+        relay_step(which, 0)
+    send_pair((0, 1), 0, pairs)
+    start_hops((0, 1, 2), 1)
+    for p in range(pairs, 0, -1):
+        send_pair((2,), 0, p)
+    forward_own(0)
+
+    def first_step(p, c):
+        forward(0, beside_first, p)
         return c
 
-    lax.fori_loop(1, frames_axis, text_step, 0)
-    send_all((2,), 0, True)
-    forward(0)
-
-    for h in range(1, heads):
-        send_all((0, 1), h)
+    lax.fori_loop(1, pairs + 1, first_step, 0)
+    forward_from(0, peers // 2)
+    for which in range(3):
+        relay_step(which, 1)
+    forward_own(1)
+
     rest = text.at[pl.ds(1, frames_axis - 1)]
     all_text = pltpu.make_async_remote_copy(
         src_ref=rest, dst_ref=rest, send_sem=text_send, recv_sem=text_recv, device_id={"tm": nxt}
     )
     all_text.wait()
     for h in range(heads):
-        lane = slice(h * DH, (h + 1) * DH)
-        lane_v = slice((heads + h) * DH, (heads + h + 1) * DH)
-        text_k[h] = text[:, :, lane].reshape(-1, DH).astype(jnp.bfloat16)
-        text_v[h] = text[:, :, lane_v].reshape(-1, DH).astype(jnp.bfloat16)
+        both = text[:, :, h * DH : (h + 1) * DH].astype(jnp.float32)
+        text_k[h] = both[:, :text_rows].reshape(-1, DH).astype(jnp.bfloat16)
+        text_v[h] = both[:, text_rows:].reshape(-1, DH).astype(jnp.bfloat16)
 
     scale = LOG2E / math.sqrt(DH)
     rows = ZT * cells
@@ -250,6 +272,7 @@
     def tile(h, a, start, count):
         n = count * cells
         chunks = [(c, min(256, n - c)) for c in range(0, n, 256)]
+        wide_chunks = [(0, 512), (512, n - 512)]
         q = qh[h, pl.ds(ZT * a, ZT)].reshape(rows, DH)
         s = product(q, text_k[h])
         place = lax.broadcasted_iota(jnp.int32, s.shape, 1)
@@ -267,21 +290,23 @@
             top = jnp.maximum(top, part + bias[t])
         top = jnp.broadcast_to(jnp.max(top, 1, keepdims=True) * scale, (rows, DH))
 
-        acc = jnp.dot(
-            weights_of(text_s[...], top),
-            jnp.concatenate([text_v[h], ones[: text_v.shape[1]]], 1),
-            preferred_element_type=jnp.float32,
-        )
-        for t in range(3):
-            shift = top - bias[t]
-            for c, w in chunks:
-                weights[t, :, c : c + w] = weights_of(scores[t, :, c : c + w], shift)
-            v = kv[t, h, pl.ds(start, count), 1].reshape(n, DH)
-            acc = acc + jnp.dot(
-                weights[t, :, :n],
-                jnp.concatenate([v, ones[:n]], 1),
-                preferred_element_type=jnp.float32,
-            )
+        pieces = [(t, c, w) for t in range(3) for c, w in wide_chunks]
+        values = [kv[t, h, pl.ds(start, count), 1].reshape(n, DH) for t in range(3)]
+        shifts = [top - b for b in bias]
+
+        def value_product(p, v):
+            both = jnp.concatenate([v, ones[: v.shape[0]]], 1)
+            return jnp.dot(p, both, preferred_element_type=jnp.float32)
+
+        acc = None
+        held = weights_of(text_s[...], top)
+        held_v = text_v[h]
+        for t, c, w in pieces:
+            p = weights_of(scores[t, :, c : c + w], shifts[t])
+            part = value_product(held, held_v)
+            acc = part if acc is None else acc + part
+            held, held_v = p, values[t][c : c + w]
+        acc = acc + value_product(held, held_v)
         oh[h, pl.ds(ZT * a, ZT)] = (
             (acc[:, :DH] / acc[:, DH:]).astype(jnp.bfloat16).reshape(ZT, cells, DH)
         )
@@ -319,8 +344,7 @@
 
             @pl.when(z == opposite)
             def _():
-                for side in range(2):
-                    hop(3, h, side).start()
+                start_hops((3,), h)
 
             @pl.when(z == me_z)
             def _():
@@ -339,12 +363,6 @@
                 own(2, h).wait()
 
     for h in range(heads):
-        if h > 0:
-            forward(h)
-        if h + 1 < heads:
-            send_all((2,), h + 1, True)
-        relay_step(2, h)
-
         def halo_step(z, c, h=h):
             for side in range(2):
                 halo(h, z, side).wait_recv()
@@ -359,10 +377,15 @@
             low = a == 0
             at_edge = jnp.logical_or(low, a == tiles - 1)
             wait_queries(h, a)
-
-            @pl.when(i == 2)
-            def _():
-                relay_step(3, h)
+            if h == 1:
+
+                @pl.when(i == 1)
+                def _():
+                    relay_step(3, 0)
+
+                @pl.when(i == 3)
+                def _():
+                    relay_step(3, 1)
 
             @pl.when(at_edge)
             def _():
@@ -373,6 +396,14 @@
                 tile(h, a, (a - 1) * ZT, 3 * ZT)
 
             send_tile(h, a)
+            if h == 0:
+                @pl.when(i < pairs)
+                def _():
+                    forward(1, beside_last, i + 1)
+
+                @pl.when(i == pairs)
+                def _():
+                    forward_from(1, peers // 2)
             return c
 
         lax.fori_loop(0, tiles, tile_step, 0)
@@ -380,16 +411,16 @@
     for h in range(heads):
         result_own(h).wait()
 
-        def end_step(j, c, h=h):
-            d = offset(j)
-            z = lax.rem(me_z + d, peers)
-            for which in range(3):
-                a2a(which, h, d, z).wait_send()
-            result(h, z).wait_send()
-            result_arrival(h, z).wait_recv()
+        def end_step(p, c, h=h):
+            for d in offsets(p):
+                z = lax.rem(me_z + d, peers)
+                for which in range(3):
+                    a2a(which, h, d, z).wait_send()
+                result(h, z).wait_send()
+                result_arrival(h, z).wait_recv()
             return c
 
-        lax.fori_loop(1, peers - 1, end_step, 0)
+        lax.fori_loop(1, pairs + 1, end_step, 0)
         result_arrival(h, opposite).wait_recv()
         for which in range(4):
             for side in range(2):
@@ -426,12 +457,11 @@
             pltpu.VMEM((heads, peers, cells, DH), jnp.bfloat16),
             pltpu.VMEM((heads, peers, cells, DH), jnp.bfloat16),
             pltpu.VMEM((heads, 4, 2, cells // 2, DH), jnp.bfloat16),
-            pltpu.VMEM((frames_axis, text_rows, 2 * heads * DH), jnp.float32),
+            pltpu.VMEM((frames_axis, 2 * text_rows, heads * DH), jnp.bfloat16),
             pltpu.VMEM((heads, frames_axis * text_rows, DH), jnp.bfloat16),
             pltpu.VMEM((heads, frames_axis * text_rows, DH), jnp.bfloat16),
             pltpu.VMEM((ZT * cells, frames_axis * text_rows), jnp.float32),
             pltpu.VMEM((3, ZT * cells, 3 * ZT * cells), jnp.float32),
-            pltpu.VMEM((3, ZT * cells, 3 * ZT * cells), jnp.bfloat16),
             dma((heads, 3, peers)),
             dma((heads, 3, peers)),
             dma((heads, 2, peers)),

time: 113 us -> 92.7 us (0.82)
  Pallas kernels: 110 us -> 89.8 us
    pallas_call x1, Pallas kernels: 110 us -> 89.8 us  [per_device(): pl.pallas_call(functools.partial(kernel, peers, frames_axis, heads, cells...]
where the time goes in v6:
time: 92.7 us; the launch traced here: 92.5 us
  Pallas kernels  89.8 us (97%)
  local copies, waits for them, and re-layouts  2.09 us (2%)
    pallas_call x1, Pallas kernels, per_device(): pl.pallas_call(functools.partial(kernel, peers, frames_axis, heads, cells...  89.8 us
    unnamed x1, local copies, waits for them, and re-layouts  2.09 us

profile of v6, /device:TPU:1, one launch (start us, length us, event | category | flops | bytes accessed | tf_op | source)
XLA Modules:
  0.0 92.5 jit_solution(17147302578257974538)
XLA Ops:
  0.7 89.8 %shard_map.64 = bf16[192,2048]{1,0:T(8,128)(2,1)} custom-call(bf16[192,2048]{1,0:T(8,128)(2,1)} %bitcast.5, bf16[192,2048]{1,0:T(8,128)(2,1)} %bitcast.6, bf16[192,2048]{1,0:T(8,128)(2,1)} %bitcast.7, bf16[8,256]{1,0:T(8,128)(2,1)} %tk_ref.1, bf16[8,256]{1,0:T(8,128)(2,1)} %tv_ref.1, s32[1]{0:T(128)S(6)} %copy.8.len_ref), custom_call_target="tpu_custom_call" | custom-call | flops 5000000000 | bytes 4000000 | tf_op jit(solution)/shard_map/pallas_call | solution.py:450
  90.5 2.1 %copy.9 = bf16[6,4,8,2048]{3,2,1,0:T(8,128)(2,1)} copy(bf16[6,4,8,2048]{3,2,1,0:T(8,128)(2,1)} %bitcast.4) | data formatting | bytes 1572864

commit v7 on v5

--- a/solution.py
+++ b/solution.py
@@ -160,7 +160,7 @@
         lax.fori_loop(start, jnp.minimum(start + share, frames_axis), step, 0)
 
     def beside_last(j):
-        send((2,), 1, offset(peers - j))
+        pass
 
     for h in range(heads):
         for which in range(3):
@@ -176,6 +176,12 @@
     lax.fori_loop(1, peers, first_queries, 0)
     forward_own(0)
     forward(0, beside_first, 1, peers)
+
+    def last_queries(j, c):
+        send((2,), 1, offset(peers - j))
+        return c
+
+    lax.fori_loop(1, peers, last_queries, 0)
     forward_own(1)
 
     rest = text.at[pl.ds(1, frames_axis - 1)]
@@ -195,7 +201,6 @@
         jnp.float32(0.0),
         jnp.where(me_t == frames_axis - 1, -jnp.inf, 0.0).astype(jnp.float32),
     )
-    ones = jnp.ones((3 * ZT * cells, DH), jnp.bfloat16)
 
     def product(q, k):
         return lax.dot_general(q, k, (((1,), (1,)), ((), ())), preferred_element_type=jnp.float32)
@@ -206,10 +211,10 @@
 
     def weights_of(s, shift):
         parts = [
-            jnp.exp2(s[:, i : i + DH] * scale - shift).astype(jnp.bfloat16)
-            for i in range(0, s.shape[1], DH)
+            jnp.exp2(s[:, i : i + DH] * scale - shift) for i in range(0, s.shape[1], DH)
         ]
-        return jnp.concatenate(parts, 1)
+        rounded = jnp.concatenate([p.astype(jnp.bfloat16) for p in parts], 1)
+        return rounded, functools.reduce(jnp.add, parts)
 
     def tile(h, a, start, count):
         n = count * cells
@@ -237,21 +242,20 @@
         shifts = [top - b for b in bias]
 
         def value_product(p, v):
-            both = jnp.concatenate([v, ones[: v.shape[0]]], 1)
-            return jnp.dot(p, both, preferred_element_type=jnp.float32)
+            return jnp.dot(p, v, preferred_element_type=jnp.float32)
 
         acc = None
-        held = weights_of(text_s[...], top)
+        held, total = weights_of(text_s[...], top)
         held_v = text_v[h]
         for t, c, w in pieces:
-            p = weights_of(scores[t, :, c : c + w], shifts[t])
+            p, sums = weights_of(scores[t, :, c : c + w], shifts[t])
+            total = total + sums
             part = value_product(held, held_v)
             acc = part if acc is None else acc + part
             held, held_v = p, values[t][c : c + w]
         acc = acc + value_product(held, held_v)
-        oh[h, pl.ds(ZT * a, ZT)] = (
-            (acc[:, :DH] / acc[:, DH:]).astype(jnp.bfloat16).reshape(ZT, cells, DH)
-        )
+        total = jnp.sum(total, 1, keepdims=True)
+        oh[h, pl.ds(ZT * a, ZT)] = (acc / total).astype(jnp.bfloat16).reshape(ZT, cells, DH)
 
     def result(h, z):
         return pltpu.make_async_remote_copy(
@@ -317,8 +321,8 @@
 
             send_tile(h, a)
             if h == 0:
-                begin = 1 + 2 * i
-                forward(1, beside_last, begin, jnp.minimum(begin + 2, peers))
+                begin = 1 + 3 * i
+                forward(1, beside_last, begin, jnp.minimum(begin + 3, peers))
             return c
 
         lax.fori_loop(0, tiles, tile_step, 0)

time: 93.6 us -> 90.4 us (0.966)
  Pallas kernels: 89.8 us -> 87.4 us
    pallas_call x1, Pallas kernels: 89.8 us -> 87.4 us  [per_device(): pl.pallas_call(functools.partial(kernel, peers, frames_axis, heads, cells...]
where the time goes in v7:
time: 90.4 us; the launch traced here: 90.2 us
  Pallas kernels  87.4 us (97%)
  local copies, waits for them, and re-layouts  2.09 us (2%)
    pallas_call x1, Pallas kernels, per_device(): pl.pallas_call(functools.partial(kernel, peers, frames_axis, heads, cells...  87.4 us
    unnamed x1, local copies, waits for them, and re-layouts  2.09 us

profile of v7, /device:TPU:1, one launch (start us, length us, event | category | flops | bytes accessed | tf_op | source)
XLA Modules:
  0.0 90.2 jit_solution(5232486692033947824)
XLA Ops:
  0.7 87.4 %shard_map.64 = bf16[192,2048]{1,0:T(8,128)(2,1)} custom-call(bf16[192,2048]{1,0:T(8,128)(2,1)} %bitcast.5, bf16[192,2048]{1,0:T(8,128)(2,1)} %bitcast.6, bf16[192,2048]{1,0:T(8,128)(2,1)} %bitcast.7, bf16[8,256]{1,0:T(8,128)(2,1)} %tk_ref.1, bf16[8,256]{1,0:T(8,128)(2,1)} %tv_ref.1, s32[1]{0:T(128)S(6)} %copy.8.len_ref), custom_call_target="tpu_custom_call" | custom-call | flops 5000000000 | bytes 4000000 | tf_op jit(solution)/shard_map/pallas_call | solution.py:370
  88.1 2.1 %copy.9 = bf16[6,4,8,2048]{3,2,1,0:T(8,128)(2,1)} copy(bf16[6,4,8,2048]{3,2,1,0:T(8,128)(2,1)} %bitcast.4) | data formatting | bytes 1572864

commit v8 on v7

--- a/solution.py
+++ b/solution.py
@@ -218,8 +218,6 @@
 
     def tile(h, a, start, count):
         n = count * cells
-        chunks = [(c, min(256, n - c)) for c in range(0, n, 256)]
-        wide_chunks = [(0, 512), (512, n - 512)]
         q = qh[h, pl.ds(ZT * a, ZT)].reshape(rows, DH)
         s = product(q, text_k[h])
         place = lax.broadcasted_iota(jnp.int32, s.shape, 1)
@@ -228,16 +226,11 @@
         top = lanes_max(s)
         for t in range(3):
             k = kv[t, h, pl.ds(start, count), 0].reshape(n, DH)
-            part = None
-            for c, w in chunks:
-                s = product(q, k[c : c + w])
-                scores[t, :, c : c + w] = s
-                m = lanes_max(s)
-                part = m if part is None else jnp.maximum(part, m)
-            top = jnp.maximum(top, part + bias[t])
+            s = product(q, k)
+            scores[t, :, :n] = s
+            top = jnp.maximum(top, lanes_max(s) + bias[t])
         top = jnp.broadcast_to(jnp.max(top, 1, keepdims=True) * scale, (rows, DH))
 
-        pieces = [(t, c, w) for t in range(3) for c, w in wide_chunks]
         values = [kv[t, h, pl.ds(start, count), 1].reshape(n, DH) for t in range(3)]
         shifts = [top - b for b in bias]
 
@@ -247,12 +240,12 @@
         acc = None
         held, total = weights_of(text_s[...], top)
         held_v = text_v[h]
-        for t, c, w in pieces:
-            p, sums = weights_of(scores[t, :, c : c + w], shifts[t])
+        for t in range(3):
+            p, sums = weights_of(scores[t, :, :n], shifts[t])
             total = total + sums
             part = value_product(held, held_v)
             acc = part if acc is None else acc + part
-            held, held_v = p, values[t][c : c + w]
+            held, held_v = p, values[t]
         acc = acc + value_product(held, held_v)
         total = jnp.sum(total, 1, keepdims=True)
         oh[h, pl.ds(ZT * a, ZT)] = (acc / total).astype(jnp.bfloat16).reshape(ZT, cells, DH)

time: 90.4 us -> 90.4 us (level)
  no operation moved by 1% of the time
where the time goes in v8:
time: 90.4 us; the launch traced here: 90.2 us
  Pallas kernels  87.4 us (97%)
  local copies, waits for them, and re-layouts  2.09 us (2%)
    pallas_call x1, Pallas kernels, per_device(): pl.pallas_call(functools.partial(kernel, peers, frames_axis, heads, cells...  87.4 us
    unnamed x1, local copies, waits for them, and re-layouts  2.09 us

profile of v8, /device:TPU:1, one launch (start us, length us, event | category | flops | bytes accessed | tf_op | source)
XLA Modules:
  0.0 90.2 jit_solution(12581493166973477948)
XLA Ops:
  0.7 87.4 %shard_map.64 = bf16[192,2048]{1,0:T(8,128)(2,1)} custom-call(bf16[192,2048]{1,0:T(8,128)(2,1)} %bitcast.5, bf16[192,2048]{1,0:T(8,128)(2,1)} %bitcast.6, bf16[192,2048]{1,0:T(8,128)(2,1)} %bitcast.7, bf16[8,256]{1,0:T(8,128)(2,1)} %tk_ref.1, bf16[8,256]{1,0:T(8,128)(2,1)} %tv_ref.1, s32[1]{0:T(128)S(6)} %copy.8.len_ref), custom_call_target="tpu_custom_call" | custom-call | flops 5000000000 | bytes 4000000 | tf_op jit(solution)/shard_map/pallas_call | solution.py:363
  88.1 2.1 %copy.9 = bf16[6,4,8,2048]{3,2,1,0:T(8,128)(2,1)} copy(bf16[6,4,8,2048]{3,2,1,0:T(8,128)(2,1)} %bitcast.4) | data formatting | bytes 1572864

commit v9 on v8

--- a/solution.py
+++ b/solution.py
@@ -51,7 +51,8 @@
     prv = lax.rem(me_t + frames_axis - 1, frames_axis)
 
     def offset(j):
-        return jnp.where(lax.rem(j, 2) == 1, (j + 1) // 2, peers - j // 2)
+        d = jnp.where(lax.rem(j, 2) == 1, (j + 1) // 2, peers - j // 2)
+        return jnp.where(lax.rem(me_t, 2) == 0, d, peers - d)
 
     def columns(z, h):
         return pl.ds(pl.multiple_of((z * heads + h) * DH, DH), DH)

time: 90.4 us -> 90.5 us (level)
  no operation moved by 1% of the time
where the time goes in v9:
time: 90.5 us; the launch traced here: 90.2 us
  Pallas kernels  87.5 us (97%)
  local copies, waits for them, and re-layouts  2.09 us (2%)
    pallas_call x1, Pallas kernels, per_device(): pl.pallas_call(functools.partial(kernel, peers, frames_axis, heads, cells...  87.5 us
    unnamed x1, local copies, waits for them, and re-layouts  2.09 us

profile of v9, /device:TPU:1, one launch (start us, length us, event | category | flops | bytes accessed | tf_op | source)
XLA Modules:
  0.0 90.2 jit_solution(16469247189235635685)
XLA Ops:
  0.7 87.5 %shard_map.64 = bf16[192,2048]{1,0:T(8,128)(2,1)} custom-call(bf16[192,2048]{1,0:T(8,128)(2,1)} %bitcast.5, bf16[192,2048]{1,0:T(8,128)(2,1)} %bitcast.6, bf16[192,2048]{1,0:T(8,128)(2,1)} %bitcast.7, bf16[8,256]{1,0:T(8,128)(2,1)} %tk_ref.1, bf16[8,256]{1,0:T(8,128)(2,1)} %tv_ref.1, s32[1]{0:T(128)S(6)} %copy.8.len_ref), custom_call_target="tpu_custom_call" | custom-call | flops 5000000000 | bytes 4000000 | tf_op jit(solution)/shard_map/pallas_call | solution.py:364
  88.1 2.1 %copy.9 = bf16[6,4,8,2048]{3,2,1,0:T(8,128)(2,1)} copy(bf16[6,4,8,2048]{3,2,1,0:T(8,128)(2,1)} %bitcast.4) | data formatting | bytes 1572864
